TPU v7x, 32 devices: a whole 2x2x4 slice. The times are simulated.
32 devices in a mesh: dp: 4 (over y, x), expert: 8 (over z, core).
Axes of the slice: x: 2, y: 2, z: 4, core: 2. Of those that a mesh axis runs over, the one named last changes fastest.
Arguments:
- tokens: bfloat16 [16384, 1024], P(('dp', 'expert')), may hold values from -6 to 6
- routes: int32 [16384, 2], P(('dp', 'expert')), may hold values from 0 to 7, all different within a row
- rel_bucket: int32 [1023], replicated, may hold values from 0 to 31
- norm_gain1: float32 [1024], replicated, may hold values from 0.25 to 1.75
- w_qkv: bfloat16 [1024, 3072], P(('dp', 'expert')), may hold values from -0.1875 to 0.1875
- w_out_proj: bfloat16 [1024, 1024], P(('dp', 'expert')), may hold values from -1.5 to 1.5
- bias_table: float32 [32, 16], replicated, may hold values from -4 to 4
- norm_gain2: float32 [1024], replicated, may hold values from 0.25 to 1.75
- w_router: float32 [1024, 8], replicated, may hold values from -0.125 to 0.125
- w_expert_in: bfloat16 [8, 2, 1024, 2816], P('expert'), may hold values from -0.1875 to 0.1875
- w_expert_out: bfloat16 [8, 2816, 1024], P('expert'), may hold values from -0.15625 to 0.15625
- grad_out: bfloat16 [16384, 1024], P(('dp', 'expert')), may hold values from -6 to 6
Outputs:
- block_out: bfloat16 [16384, 1024], P(('dp', 'expert'))
- grad_tokens: float32 [16384, 1024], P(('dp', 'expert'))
- grad_norm1: float32 [1024], replicated
- grad_qkv: float32 [1024, 3072], P(('dp', 'expert'))
- grad_out_proj: float32 [1024, 1024], P(('dp', 'expert'))
- grad_bias: float32 [32, 16], replicated
- grad_norm2: float32 [1024], replicated
- grad_router: float32 [1024, 8], replicated
- grad_expert_in: float32 [8, 2, 1024, 2816], P('expert', None, 'dp')
- grad_expert_out: float32 [8, 2816, 1024], P('expert', None, 'dp')
Inputs may be any that keep to these rules, and one draw needn't show every extreme that they name: `routes`: each token names two different experts, and every expert is named by some token.
All inputs are finite; a program needn't handle non-finite values.
Results may differ from a plain program's by a relative error of at most 0.015.
Values may be sent and summed in bfloat16 or wider, within the bound.
A program may use at most 256 MiB of HBM per device.

v0:
```python
import jax
import jax.numpy as jnp
from jax import lax
from jax.sharding import PartitionSpec as P

LENGTH = 512


EPS = 1e-06


def rms_forward(values, norm_gain):
    inv_rms = lax.rsqrt(jnp.mean(values * values, axis=-1, keepdims=True) + EPS)
    return (values * inv_rms * norm_gain, inv_rms)


def rms_backward(values, inv_rms, norm_gain, grad_norm):
    normed = values * inv_rms
    scaled = grad_norm * norm_gain
    grad_gain = jnp.sum(grad_norm * normed, axis=0)
    grad_values = inv_rms * (scaled - normed * jnp.mean(scaled * normed, axis=-1, keepdims=True))
    return (grad_values, grad_gain)


def split_heads(seq_block, head_count):
    length = seq_block.shape[0]
    model_width = seq_block.shape[1] // 3
    head_size = model_width // head_count
    query_rows = seq_block[:, :model_width].reshape(length, head_count, head_size)
    key_rows = seq_block[:, model_width : 2 * model_width].reshape(length, head_count, head_size)
    value_rows = seq_block[:, 2 * model_width :].reshape(length, head_count, head_size)
    return (query_rows, key_rows, value_rows, head_size ** (-0.5))


def attend(seq_block, bias_full, head_count):
    query_rows, key_rows, value_rows, scale_factor = split_heads(seq_block, head_count)
    scores = (
        jnp.einsum("qhd,khd->hqk", query_rows, key_rows, preferred_element_type=jnp.float32)
        * scale_factor
        + bias_full
    )
    row_max = jnp.max(scores, axis=-1, keepdims=True)
    exp_scores = jnp.exp(scores - row_max)
    row_total = jnp.sum(exp_scores, axis=-1, keepdims=True)
    attn_probs = (exp_scores / row_total).astype(jnp.bfloat16)
    mixed_out = jnp.einsum(
        "hqk,khd->qhd", attn_probs, value_rows, preferred_element_type=jnp.float32
    )
    return (mixed_out.reshape(seq_block.shape[0], -1), (row_max + jnp.log(row_total))[..., 0])


def attend_back(seq_block, grad_mixed, log_total, bias_full, head_count):
    query_rows, key_rows, value_rows, scale_factor = split_heads(seq_block, head_count)
    length = seq_block.shape[0]
    grad_heads = grad_mixed.reshape(length, head_count, -1)
    scores = (
        jnp.einsum("qhd,khd->hqk", query_rows, key_rows, preferred_element_type=jnp.float32)
        * scale_factor
        + bias_full
    )
    attn_probs = jnp.exp(scores - log_total[..., None])
    grad_probs = jnp.einsum(
        "qhd,khd->hqk", grad_heads, value_rows, preferred_element_type=jnp.float32
    )
    row_delta = jnp.sum(attn_probs * grad_probs, axis=-1, keepdims=True)
    grad_scores = (attn_probs * (grad_probs - row_delta)).astype(jnp.bfloat16)
    grad_query = (
        jnp.einsum("hqk,khd->qhd", grad_scores, key_rows, preferred_element_type=jnp.float32)
        * scale_factor
    )
    grad_key = (
        jnp.einsum("hqk,qhd->khd", grad_scores, query_rows, preferred_element_type=jnp.float32)
        * scale_factor
    )
    grad_value = jnp.einsum(
        "hqk,qhd->khd",
        attn_probs.astype(jnp.bfloat16),
        grad_heads,
        preferred_element_type=jnp.float32,
    )
    grad_block = jnp.concatenate(
        [
            grad_query.reshape(length, -1),
            grad_key.reshape(length, -1),
            grad_value.reshape(length, -1),
        ],
        axis=1,
    )
    return (grad_block, grad_scores)


def shards(
    tokens,
    routes,
    rel_bucket,
    norm_gain1,
    w_qkv,
    w_out_proj,
    bias_table,
    norm_gain2,
    w_router,
    w_expert_in,
    w_expert_out,
    grad_out,
):
    highest = lax.Precision.HIGHEST
    row_count, model_width = tokens.shape
    bucket_count, head_count = bias_table.shape
    length = LENGTH
    seq_count = row_count // length
    expert_count = lax.axis_size("expert")
    capacity = 10 * row_count // (4 * expert_count)
    slot_total = expert_count * capacity
    qkv_full, out_full = (
        lax.all_gather(w_qkv, ("dp", "expert"), axis=0, tiled=True),
        lax.all_gather(w_out_proj, ("dp", "expert"), axis=0, tiled=True),
    )
    inputs_f = tokens.astype(jnp.float32)
    normed1, inv_rms1 = rms_forward(inputs_f, norm_gain1)
    normed1_r = normed1.astype(jnp.bfloat16)
    qkv_r = jnp.dot(normed1_r, qkv_full, preferred_element_type=jnp.float32).astype(jnp.bfloat16)
    positions = jnp.arange(length, dtype=jnp.int32)
    distance = positions[:, None] - positions[None, :] + length - 1
    bucket_pos = jnp.take(rel_bucket, distance.reshape(-1))
    bucket_ids = jnp.arange(bucket_count, dtype=jnp.int32)
    position_hot = (bucket_ids[:, None] == bucket_pos[None, :]).astype(jnp.float32)
    bias_full = jnp.dot(bias_table.T, position_hot, precision=highest).reshape(
        head_count, length, length
    )
    seq_blocks = qkv_r.reshape(seq_count, length, 3 * model_width)

    def attend_one(seq_block):
        return attend(seq_block, bias_full, head_count)

    mixed_all, log_totals = lax.map(attend_one, seq_blocks)
    mixed_r = mixed_all.reshape(row_count, model_width).astype(jnp.bfloat16)
    residual = inputs_f + jnp.dot(mixed_r, out_full, preferred_element_type=jnp.float32)
    normed2, inv_rms2 = rms_forward(residual, norm_gain2)
    normed2_r = normed2.astype(jnp.bfloat16)
    normed2_f = normed2_r.astype(jnp.float32)
    logits = jnp.dot(normed2_f, w_router, precision=highest)
    expert_ids = jnp.arange(expert_count, dtype=jnp.int32)
    route_hot = (routes[:, :, None] == expert_ids[None, None, :]).astype(jnp.float32)
    chosen = jnp.einsum("te,tce->tc", logits, route_hot, precision=highest)
    gate_probs = jax.nn.softmax(chosen, axis=-1)
    pair_expert = routes.T.reshape(2 * row_count)
    pair_hot = (pair_expert[:, None] == expert_ids[None, :]).astype(jnp.int32)
    slot_place = jnp.sum((jnp.cumsum(pair_hot, axis=0) - 1) * pair_hot, axis=1)
    kept_mask = slot_place < capacity
    slot_index = jnp.where(kept_mask, pair_expert * capacity + slot_place, slot_total)
    fetch_index = jnp.minimum(slot_index, slot_total - 1)
    kept_f = kept_mask.astype(jnp.float32)[:, None]
    source_rows = jnp.concatenate([normed2_r, normed2_r], axis=0)
    outgoing = (
        jnp.zeros((slot_total, model_width), jnp.bfloat16)
        .at[slot_index]
        .set(source_rows, mode="drop")
    )
    arrived = lax.all_to_all(
        outgoing.reshape(expert_count, capacity, model_width),
        "expert",
        split_axis=0,
        concat_axis=0,
        tiled=True,
    ).reshape(slot_total, model_width)
    w_in = w_expert_in[0]
    w_out = w_expert_out[0]
    gate_pre = jnp.dot(arrived, w_in[0], preferred_element_type=jnp.float32)
    up_pre = jnp.dot(arrived, w_in[1], preferred_element_type=jnp.float32)
    gelu_val, gelu_back = jax.vjp(jax.nn.gelu, gate_pre)
    hidden_r = (gelu_val * up_pre).astype(jnp.bfloat16)
    produced = jnp.dot(hidden_r, w_out, preferred_element_type=jnp.float32).astype(jnp.bfloat16)
    returned = lax.all_to_all(
        produced.reshape(expert_count, capacity, model_width),
        "expert",
        split_axis=0,
        concat_axis=0,
        tiled=True,
    ).reshape(slot_total, model_width)
    paired = returned[fetch_index].astype(jnp.float32) * kept_f
    first_out = paired[:row_count]
    second_out = paired[row_count:]
    block_out = (
        residual + gate_probs[:, 0:1] * first_out + gate_probs[:, 1:2] * second_out
    ).astype(jnp.bfloat16)
    grad_y = grad_out.astype(jnp.float32)
    grad_gates = jnp.stack(
        [jnp.sum(grad_y * first_out, axis=-1), jnp.sum(grad_y * second_out, axis=-1)], axis=1
    )
    grad_chosen = gate_probs * (
        grad_gates - jnp.sum(gate_probs * grad_gates, axis=-1, keepdims=True)
    )
    grad_logits = jnp.einsum("tc,tce->te", grad_chosen, route_hot, precision=highest)
    grad_router = jnp.dot(normed2_f.T, grad_logits, precision=highest)
    back_rows = jnp.concatenate(
        [gate_probs[:, 0:1] * grad_y, gate_probs[:, 1:2] * grad_y], axis=0
    ).astype(jnp.bfloat16)
    back_slots = (
        jnp.zeros((slot_total, model_width), jnp.bfloat16)
        .at[slot_index]
        .set(back_rows, mode="drop")
    )
    grad_produced = lax.all_to_all(
        back_slots.reshape(expert_count, capacity, model_width),
        "expert",
        split_axis=0,
        concat_axis=0,
        tiled=True,
    ).reshape(slot_total, model_width)
    grad_hidden = jnp.dot(grad_produced, w_out.T, preferred_element_type=jnp.float32)
    grad_w_out = jnp.dot(hidden_r.T, grad_produced, preferred_element_type=jnp.float32)
    grad_gate_r = gelu_back(grad_hidden * up_pre)[0].astype(jnp.bfloat16)
    grad_up_r = (grad_hidden * gelu_val).astype(jnp.bfloat16)
    grad_w_in = jnp.stack(
        [
            jnp.dot(arrived.T, grad_gate_r, preferred_element_type=jnp.float32),
            jnp.dot(arrived.T, grad_up_r, preferred_element_type=jnp.float32),
        ],
        axis=0,
    )
    grad_arrived = (
        jnp.dot(grad_gate_r, w_in[0].T, preferred_element_type=jnp.float32)
        + jnp.dot(grad_up_r, w_in[1].T, preferred_element_type=jnp.float32)
    ).astype(jnp.bfloat16)
    grad_returned = lax.all_to_all(
        grad_arrived.reshape(expert_count, capacity, model_width),
        "expert",
        split_axis=0,
        concat_axis=0,
        tiled=True,
    ).reshape(slot_total, model_width)
    grad_pairs = grad_returned[fetch_index].astype(jnp.float32) * kept_f
    grad_normed2 = (
        jnp.dot(grad_logits, w_router.T, precision=highest)
        + grad_pairs[:row_count]
        + grad_pairs[row_count:]
    )
    grad_res_norm, grad_gain2 = rms_backward(residual, inv_rms2, norm_gain2, grad_normed2)
    grad_residual = grad_y + grad_res_norm
    qkv_back, out_back = (qkv_full, out_full)
    grad_attn_r = grad_residual.astype(jnp.bfloat16)
    grad_out_w = jnp.dot(mixed_r.T, grad_attn_r, preferred_element_type=jnp.float32)
    grad_mixed_r = jnp.dot(grad_attn_r, out_back.T, preferred_element_type=jnp.float32).astype(
        jnp.bfloat16
    )

    def back_step(score_sum, packed):
        seq_block, grad_mixed, log_total = packed
        grad_block, grad_scores = attend_back(
            seq_block, grad_mixed, log_total, bias_full, head_count
        )
        return (score_sum + grad_scores.astype(jnp.float32), grad_block)

    score_init = jnp.zeros((head_count, length, length), jnp.float32)
    score_sum, grad_blocks = lax.scan(
        back_step,
        score_init,
        (seq_blocks, grad_mixed_r.reshape(seq_count, length, model_width), log_totals),
    )
    grad_qkv_r = grad_blocks.reshape(row_count, 3 * model_width).astype(jnp.bfloat16)
    grad_qkv_w = jnp.dot(normed1_r.T, grad_qkv_r, preferred_element_type=jnp.float32)
    grad_normed1 = jnp.dot(grad_qkv_r, qkv_back.T, preferred_element_type=jnp.float32)
    grad_in_norm, grad_gain1 = rms_backward(inputs_f, inv_rms1, norm_gain1, grad_normed1)
    grad_tokens = grad_residual + grad_in_norm
    grad_bias_local = jnp.dot(
        position_hot, score_sum.reshape(head_count, length * length).T, precision=highest
    )
    grad_bias, grad_norm1, grad_norm2, grad_router_all = lax.psum(
        (grad_bias_local, grad_gain1, grad_gain2, grad_router), ("dp", "expert")
    )
    grad_qkv, grad_out_proj = (
        lax.psum_scatter(grad_qkv_w, ("dp", "expert"), scatter_dimension=0, tiled=True),
        lax.psum_scatter(grad_out_w, ("dp", "expert"), scatter_dimension=0, tiled=True),
    )
    grad_expert_in, grad_expert_out = (
        lax.psum_scatter(
            grad_w_in[None].astype(jnp.bfloat16), "dp", scatter_dimension=2, tiled=True
        ).astype(jnp.float32),
        lax.psum_scatter(
            grad_w_out[None].astype(jnp.bfloat16), "dp", scatter_dimension=2, tiled=True
        ).astype(jnp.float32),
    )
    return (
        block_out,
        grad_tokens,
        grad_norm1,
        grad_qkv,
        grad_out_proj,
        grad_bias,
        grad_norm2,
        grad_router_all,
        grad_expert_in,
        grad_expert_out,
    )


def solution(mesh):
    in_specs = (
        P(("dp", "expert"), None),
        P(("dp", "expert"), None),
        P(),
        P(),
        P(("dp", "expert"), None),
        P(("dp", "expert"), None),
        P(),
        P(),
        P(),
        P("expert", None, None, None),
        P("expert", None, None),
        P(("dp", "expert"), None),
    )
    out_specs = (
        P(("dp", "expert"), None),
        P(("dp", "expert"), None),
        P(),
        P(("dp", "expert"), None),
        P(("dp", "expert"), None),
        P(),
        P(),
        P(),
        P("expert", None, "dp", None),
        P("expert", None, "dp"),
    )
    return jax.shard_map(shards, mesh=mesh, in_specs=in_specs, out_specs=out_specs, check_vma=False)
```

profile of v0, /device:TPU:0, one launch (start us, length us, event | category | flops | bytes accessed | tf_op | source)
XLA Modules:
  0.0 3008.9 jit_solution(10341415581424221071)
XLA Ops:
  16.5 2125.1 %gather_fusion = s32[262144]{0:T(1024)} fusion(s32[1023]{0:T(1024)S(1)} %copy-done.1, s32[262144]{0:T(1024)S(1)} %broadcast_clamp_fusion), kind=kCustom, calls=%fused_computation | custom fusion | bytes 3145728 | tf_op jit(solution)/shard_map/jit(_take)/gather | solution.py:124
  2143.0 10.7 fusion.1
  2153.7 19.1 copy.58
  2172.9 18.0 copy.38
  2207.2 10.6 fusion.95
  2217.8 8.4 fusion.4
  2226.8 7.5 fusion.61
  2239.3 7.9 scatter_custom_fusion
  2247.2 66.6 %all_to_all.20 = bf16[8,160,1024]{2,1,0:T(8,128)(2,1)S(1)} all-to-all(bf16[8,160,1024]{2,1,0:T(8,128)(2,1)} %bitcast.172), channel_id=1, replica_groups=mesh['dp'=4,'expert'=8] {'expert'}, dimensions={0} | all-to-all | bytes 5242880 | tf_op jit(solution)/shard_map/all_to_all | solution.py:159
  2313.9 13.9 fusion.27
  2327.8 19.1 multiply_convert_fusion.2
  2346.9 12.6 fusion.35
  2368.8 54.5 %all-to-all-done.1 = bf16[8,160,1024]{2,1,0:T(8,128)(2,1)S(1)} async-done(((bf16[8,160,1024]{2,1,0:T(8,128)(2,1)}), bf16[8,160,1024]{2,1,0:T(8,128)(2,1)S(1)}, u32[]{:S(2)}, u32[]{:S(2)}) %all-to-all-start.1) | async-done | bytes 2621472 | tf_op jit(solution)/shard_map/all_to_all | solution.py:173
  2433.4 7.3 scatter_custom_fusion.1
  2440.7 62.8 %all_to_all.21 = bf16[8,160,1024]{2,1,0:T(8,128)(2,1)S(1)} all-to-all(bf16[8,160,1024]{2,1,0:T(8,128)(2,1)S(1)} %bitcast.171), channel_id=1, replica_groups=mesh['dp'=4,'expert'=8] {'expert'}, dimensions={0} | all-to-all | bytes 5242880 | tf_op jit(solution)/shard_map/all_to_all | solution.py:203
  2504.9 12.5 convert_bitcast_fusion
  2517.9 26.4 fusion.11
  2544.3 11.3 convert_bitcast_fusion.2
  2555.7 8.7 convert_bitcast_fusion.1
  2569.7 11.7 fusion.21
  2581.5 12.8 add_convert_fusion
  2601.2 56.9 %all-to-all-done.3 = bf16[8,160,1024]{2,1,0:T(8,128)(2,1)S(1)} async-done(((bf16[8,160,1024]{2,1,0:T(8,128)(2,1)}), bf16[8,160,1024]{2,1,0:T(8,128)(2,1)S(1)}, u32[]{:S(2)}, u32[]{:S(2)}) %all-to-all-start.3) | async-done | bytes 2621472 | tf_op jit(solution)/shard_map/all_to_all | solution.py:225
  2678.8 14.3 multiply_reduce_fusion
  2696.3 8.1 multiply_convert_fusion
  2710.1 7.0 multiply_convert_fusion.3
  2722.2 10.5 fusion.67
  2734.5 15.0 copy.62
  2749.5 8.0 fusion
  2757.6 8.2 fusion.47
  2765.8 39.8 %all-reduce = (f32[1024]{0:T(1024)}, f32[32,16]{0,1:T(8,128)}, f32[1024]{0:T(1024)}, f32[1024,8]{0,1:T(8,128)}) all-reduce(f32[1024]{0:T(1024)S(1)} %get-tuple-element.50, f32[32,16]{0,1:T(8,128)S(1)} %fusion, f32[1024]{0:T(1024)S(1)} %get-tuple-element.48, f32[1024,8]{0,1:T(8,128)S(1)} %fusion.97), channel_id=1, replica_groups=mesh['dp'=4,'expert'=8] {'dp','expert'}, use_global_device_ids=true, to_apply=%region_18.19 | all-reduce | flops 10752 | bytes 86016 | tf_op jit(solution)/shard_map/psum | solution.py:268
  2817.0 25.8 reduce-scatter.7.cloned.1.call-done
  2842.8 158.8 %reduce-scatter.5.cloned.1.call-done = f32[32,3072]{1,0:T(8,128)} async-done(((f32[1024,3072]{1,0:T(8,128)}), f32[32,3072]{1,0:T(8,128)}) %reduce-scatter.5.cloned.1.call-update) | async-done | bytes 393232 | tf_op jit(solution)/shard_map/reduce_scatter | solution.py:272
  (190 shorter events, 113.6 us)
Async XLA Ops:
  7.2 2356.4 %copy-start = (f32[1024,8]{0,1:T(8,128)S(1)}, f32[1024,8]{0,1:T(8,128)}, u32[]{:S(2)}) copy-start(f32[1024,8]{0,1:T(8,128)} %param.20) | copy-start | bytes 98308
  7.2 2186.6 %all-gather.3.cloned.1.call-start = ((), (), s32[]{:S(2)}) async-start(), calls=%async_computation.8 | async-start | bytes 6488064 | tf_op jit(solution)/shard_map/all_gather | solution.py:115
  7.9 2226.5 %all-gather.5.cloned.1.call-start = ((), (), s32[]{:S(2)}) async-start(), calls=%async_computation.9 | async-start | bytes 2162688 | tf_op jit(solution)/shard_map/all_gather | solution.py:116
  16.5 2125.1 %copy-start.25 = (s32[64,4,8,128]{3,1,2,0:T(4,128)S(1)}, s32[64,4,8,128]{3,1,2,0:T(4,128)}, u32[]{:S(2)}) copy-start(s32[64,4,8,128]{3,1,2,0:T(4,128)} %copy.54) | copy-start | bytes 3145732
  16.5 2125.1 %copy-start.26 = (s32[64,4,8,128]{3,1,2,0:T(4,128)S(1)}, s32[64,4,8,128]{3,1,2,0:T(4,128)}, u32[]{:S(2)}) copy-start(s32[64,4,8,128]{3,1,2,0:T(4,128)} %copy.55) | copy-start | bytes 3145732
  2143.0 10.7 copy-start.22
  2172.8 18.0 copy-start.37
  2172.8 21.0 copy-start.18
  2172.8 21.0 copy-start.43
  2172.9 21.0 copy-start.45
  2202.6 15.2 copy-start.13
  2204.5 13.3 copy-start.11
  2217.8 8.4 copy-start.33
  2217.8 9.0 copy-start.24
  2237.8 76.1 %copy-start.40 = (f32[512]{0:T(512)}, f32[512]{0:T(512)S(1)}, u32[]{:S(2)}) copy-start(f32[512]{0:T(512)S(1)} %add_rsqrt_fusion) | copy-start | bytes 6148
  2239.3 74.6 %copy-start.9 = (bf16[512,1024]{1,0:T(8,128)(2,1)}, bf16[512,1024]{1,0:T(8,128)(2,1)S(1)}, u32[]{:S(2)}) copy-start(bf16[512,1024]{1,0:T(8,128)(2,1)S(1)} %multiply_convert_fusion.5) | copy-start | bytes 3145732
  2313.9 13.9 copy-start.28
  2359.5 63.9 %all-to-all-start.1 = ((bf16[8,160,1024]{2,1,0:T(8,128)(2,1)}), bf16[8,160,1024]{2,1,0:T(8,128)(2,1)S(1)}, u32[]{:S(2)}, u32[]{:S(2)}) async-start(bf16[8,160,1024]{2,1,0:T(8,128)(2,1)} %bitcast.193), calls=%async_computation.1 | async-start | bytes 5242880 | tf_op jit(solution)/shard_map/all_to_all | solution.py:173
  2363.1 445.9 %reduce-scatter.11.cloned.1.call-start = ((), (), s32[]{:S(2)}) async-start(), calls=%async_computation.13 | async-start | bytes 7208960 | tf_op jit(solution)/shard_map/reduce_scatter | solution.py:279
  2517.5 294.8 %reduce-scatter.9.cloned.1.call-start = ((), (), s32[]{:S(2)}) async-start(), calls=%async_computation.12 | async-start | bytes 14417920 | tf_op jit(solution)/shard_map/reduce_scatter | solution.py:276
  2517.9 26.4 copy-start.29
  2544.3 11.4 copy-start.47
  2594.2 63.9 %all-to-all-start.3 = ((bf16[8,160,1024]{2,1,0:T(8,128)(2,1)}), bf16[8,160,1024]{2,1,0:T(8,128)(2,1)S(1)}, u32[]{:S(2)}, u32[]{:S(2)}) async-start(bf16[8,160,1024]{2,1,0:T(8,128)(2,1)} %bitcast.194), calls=%async_computation.3 | async-start | bytes 5242880 | tf_op jit(solution)/shard_map/all_to_all | solution.py:225
  2597.9 245.0 %reduce-scatter.7.cloned.1.call-start = ((), (), s32[]{:S(2)}) async-start(), calls=%async_computation.11 | async-start | bytes 4325376 | tf_op jit(solution)/shard_map/reduce_scatter | solution.py:273
  2673.5 328.1 %reduce-scatter.5.cloned.1.call-start = ((), (), s32[]{:S(2)}) async-start(), calls=%async_computation.10 | async-start | bytes 12976128 | tf_op jit(solution)/shard_map/reduce_scatter | solution.py:272
  2678.8 14.3 slice-start
  2678.8 14.5 slice-start.1
  2678.8 16.3 slice-start.2
  2678.8 17.5 slice-start.3
  2696.3 11.3 copy-start.12
  2734.5 15.0 copy-start.23
  2757.6 48.0 %copy-start.8 = (f32[512,1024]{1,0:T(8,128)S(1)}, f32[512,1024]{1,0:T(8,128)}, u32[]{:S(2)}) copy-start(f32[512,1024]{1,0:T(8,128)} %copy-done.7) | copy-start | bytes 6291460
  (28 other events, 93.0 us)
Sparse Core Ops, SparseCore 0:
  11.0 72.1 all-gather.2
  86.2 54.9 all-gather.4
  2517.6 64.6 reduce-scatter.10
  2585.3 112.1 reduce-scatter.8
  2700.1 142.6 reduce-scatter.6
  2849.3 152.2 reduce-scatter.4
where the time goes:
time: 3010 us
  local copies, waits for them, and re-layouts  2210 us (73%)
  waiting for transfers between devices  297 us (10%)
  matrix products  241 us (8%)
  blocking collectives  169 us (6%)
  other arithmetic  64.4 us (2%)
    gather x1, local copies, waits for them, and re-layouts, shards(): bucket_pos = jnp.take(rel_bucket, distance.reshape(-1))  2130 us
    reduce_scatter x1, waiting for transfers between devices, shards(): lax.psum_scatter(grad_qkv_w, ('dp', 'expert'), scatter_dimension=0, tiled...  159 us
    all_to_all x1, blocking collectives, shards(): lax.all_to_all(outgoing.reshape(expert_count, capacity, model_width), 'ex...  66.6 us
    all_to_all x1, blocking collectives, shards(): lax.all_to_all(back_slots.reshape(expert_count, capacity, model_width), '...  62.8 us
  transfers between devices with their start and end apart: 8, of which 4 were waited for; matrix products, arithmetic and copies ran while one was open for 80% of the time, Pallas kernels for 0%

commit v1 on v0

v1 whole, which is shorter than its diff:
```python
import functools

import jax
import jax.numpy as jnp
from jax import lax
from jax.experimental import pallas as pl
from jax.experimental.pallas import tpu as pltpu
from jax.sharding import PartitionSpec as P

LENGTH = 512
EPS = 1e-06
HIGHEST = lax.Precision.HIGHEST
F32 = jnp.float32
BF16 = jnp.bfloat16


def dot_nt(a, b):
    return lax.dot_general(a, b, (((1,), (1,)), ((), ())), preferred_element_type=F32)


def dot_nn(a, b):
    return jnp.dot(a, b, preferred_element_type=F32)


def iota(shape, axis):
    return lax.broadcasted_iota(jnp.int32, shape, axis)


def spread_bias(row):
    values = jnp.broadcast_to(row, (8, 1024))
    lift = 7 - iota((8, 1024), 0)
    for bit in (1, 2, 4):
        values = jnp.where((lift // bit) % 2 == 1, pltpu.roll(values, 1024 - bit, 1), values)
    return jnp.concatenate(
        [pltpu.roll(values, (904 + 8 * block) % 1024, 1) for block in range(16)], axis=0
    )


def fold_bias(parts):
    total = parts[0:8]
    total = pltpu.roll(total, 120, 1)
    for block in range(1, 16):
        piece = parts[8 * block : 8 * block + 8]
        total = total + (pltpu.roll(piece, 120 - 8 * block, 1) if block < 15 else piece)
    lift = 7 - iota((8, 1024), 0)
    for bit in (1, 2, 4):
        total = jnp.where((lift // bit) % 2 == 1, pltpu.roll(total, bit, 1), total)
    return jnp.sum(total, axis=0, keepdims=True)


def attend_pair(pair, q_ref, k_ref, v_ref, table_ref, o_ref, p_ref):
    query = q_ref[...] * jnp.asarray(0.125, BF16)
    values_t = v_ref[...].T
    half = iota((512, 128), 1) // 64
    halves = []
    for t in range(2):
        shifted = spread_bias(table_ref[pl.ds(2 * pair + t, 1), :])
        query_t = jnp.where(half == t, query, jnp.zeros_like(query))
        scores = [
            dot_nt(k_ref[128 * c : 128 * c + 128, :], query_t)
            + shifted[:, 384 - 128 * c : 896 - 128 * c]
            for c in range(4)
        ]
        top = functools.reduce(jnp.maximum, [jnp.max(s, axis=0, keepdims=True) for s in scores])
        exps = [jnp.exp(s - top) for s in scores]
        total = functools.reduce(jnp.add, [jnp.sum(e, axis=0, keepdims=True) for e in exps])
        inverse = 1.0 / total
        for c in range(4):
            p_ref[t, 128 * c : 128 * c + 128, :] = (exps[c] * inverse).astype(BF16)
        halves.append(dot_nn(values_t, p_ref[t]))
    mixed = jnp.where(iota((128, 512), 0) < 64, halves[0], halves[1])
    o_ref[...] = mixed.T.astype(BF16)


def attend_back_pair(pair, q_ref, k_ref, v_ref, p_ref, do_ref, dq_ref, dk_ref, dv_ref, fold_ref):
    query = q_ref[...] * jnp.asarray(0.125, BF16)
    keys_t = k_ref[...].T
    values = v_ref[...]
    grads = do_ref[...]
    half = iota((512, 128), 1) // 64
    dq_halves, dk_halves, dv_halves = [], [], []
    for t in range(2):
        values_t = jnp.where(half == t, values, jnp.zeros_like(values))
        probs = [p_ref[t, 128 * c : 128 * c + 128, :].astype(F32) for c in range(4)]
        grad_probs = [dot_nt(values_t[128 * c : 128 * c + 128], grads) for c in range(4)]
        delta = functools.reduce(
            jnp.add,
            [jnp.sum(p * g, axis=0, keepdims=True) for p, g in zip(probs, grad_probs)],
        )
        scores = [(p * (g - delta)).astype(BF16) for p, g in zip(probs, grad_probs)]
        padded = [
            jnp.concatenate(
                ([jnp.zeros((128, 384 - 128 * c), F32)] if c < 3 else [])
                + [scores[c].astype(F32), jnp.zeros((128, 128 + 128 * c), F32)],
                axis=1,
            )
            for c in range(4)
        ]
        fold_ref[pl.ds(2 * pair + t, 1), :] = fold_bias(functools.reduce(jnp.add, padded))
        grad_scores = jnp.concatenate(scores, axis=0)
        dv_halves.append(dot_nn(p_ref[t], grads))
        dk_halves.append(dot_nn(grad_scores, query))
        dq_halves.append(dot_nn(keys_t, grad_scores))
    dq = jnp.where(iota((128, 512), 0) < 64, dq_halves[0], dq_halves[1]) * 0.125
    dq_ref[...] = dq.T.astype(BF16)
    dk_ref[...] = jnp.where(half == 0, dk_halves[0], dk_halves[1]).astype(BF16)
    dv_ref[...] = jnp.where(half == 0, dv_halves[0], dv_halves[1]).astype(BF16)


def pair_spec(offset):
    return pl.BlockSpec((512, 128), lambda pair: (0, offset + pair))


WHOLE = pl.BlockSpec((16, 1024), lambda pair: (0, 0))
PROBS = pl.BlockSpec((2, 512, 512), lambda pair: (pair, 0, 0))
PARAMS = pltpu.CompilerParams(vmem_limit_bytes=48 * 1024 * 1024)


def attend(qkv, table):
    def body(*refs):
        attend_pair(pl.program_id(0), *refs)

    return pl.pallas_call(
        body,
        grid=(8,),
        in_specs=[pair_spec(0), pair_spec(8), pair_spec(16), WHOLE],
        out_specs=[pair_spec(0), PROBS],
        out_shape=[
            jax.ShapeDtypeStruct((512, 1024), BF16),
            jax.ShapeDtypeStruct((16, 512, 512), BF16),
        ],
        compiler_params=PARAMS,
    )(qkv, qkv, qkv, table)


def attend_back(qkv, probs, grad_mixed):
    def body(*refs):
        attend_back_pair(pl.program_id(0), *refs)

    return pl.pallas_call(
        body,
        grid=(8,),
        in_specs=[pair_spec(0), pair_spec(8), pair_spec(16), PROBS, pair_spec(0)],
        out_specs=[pair_spec(0), pair_spec(0), pair_spec(0), WHOLE],
        out_shape=[
            jax.ShapeDtypeStruct((512, 1024), BF16),
            jax.ShapeDtypeStruct((512, 1024), BF16),
            jax.ShapeDtypeStruct((512, 1024), BF16),
            jax.ShapeDtypeStruct((16, 1024), F32),
        ],
        compiler_params=PARAMS,
    )(qkv, qkv, qkv, probs, grad_mixed)


def rms_forward(values, norm_gain):
    inv_rms = lax.rsqrt(jnp.mean(values * values, axis=-1, keepdims=True) + EPS)
    return (values * inv_rms * norm_gain, inv_rms)


def rms_backward(values, inv_rms, norm_gain, grad_norm):
    normed = values * inv_rms
    scaled = grad_norm * norm_gain
    grad_gain = jnp.sum(grad_norm * normed, axis=0)
    grad_values = inv_rms * (scaled - normed * jnp.mean(scaled * normed, axis=-1, keepdims=True))
    return (grad_values, grad_gain)


def shards(
    tokens,
    routes,
    rel_bucket,
    norm_gain1,
    w_qkv,
    w_out_proj,
    bias_table,
    norm_gain2,
    w_router,
    w_expert_in,
    w_expert_out,
    grad_out,
):
    row_count, model_width = tokens.shape
    bucket_count, head_count = bias_table.shape
    expert_count = lax.axis_size("expert")
    capacity = 10 * row_count // (4 * expert_count)
    slot_total = expert_count * capacity
    qkv_full = lax.all_gather(w_qkv, ("dp", "expert"), axis=0, tiled=True)
    out_full = lax.all_gather(w_out_proj, ("dp", "expert"), axis=0, tiled=True)

    def exchange(rows):
        return lax.all_to_all(
            rows.reshape(expert_count, capacity, model_width),
            "expert",
            split_axis=0,
            concat_axis=0,
            tiled=True,
        ).reshape(slot_total, model_width)

    expert_ids = jnp.arange(expert_count, dtype=jnp.int32)
    pair_expert = routes.T.reshape(2 * row_count)
    pair_hot = pair_expert[:, None] == expert_ids[None, :]
    pair_ids = jnp.arange(2 * row_count, dtype=jnp.int32)
    earlier = (pair_ids[:, None] > pair_ids[None, :]).astype(BF16)
    counts = dot_nn(earlier, pair_hot.astype(BF16))
    slot_place = jnp.sum(jnp.where(pair_hot, counts, 0.0), axis=1).astype(jnp.int32)
    slot_index = jnp.where(
        slot_place < capacity, pair_expert * capacity + slot_place, slot_total
    ).reshape(2, row_count)
    slot_ids = jnp.arange(slot_total, dtype=jnp.int32)
    hot0 = (slot_ids[:, None] == slot_index[0][None, :]).astype(BF16)
    hot1 = (slot_ids[:, None] == slot_index[1][None, :]).astype(BF16)
    hot = hot0 + hot1

    bucket_ids = jnp.arange(bucket_count, dtype=jnp.int32)
    bucket_hot = jnp.concatenate(
        [bucket_ids[:, None] == rel_bucket[None, :], jnp.zeros((bucket_count, 1), bool)], axis=1
    ).astype(F32)
    table = jnp.dot(bias_table.T, bucket_hot, precision=HIGHEST)

    inputs_f = tokens.astype(F32)
    normed1, inv_rms1 = rms_forward(inputs_f, norm_gain1)
    normed1_r = normed1.astype(BF16)
    qkv_r = dot_nn(normed1_r, qkv_full).astype(BF16)
    mixed_r, probs = attend(qkv_r, table)
    residual = inputs_f + dot_nn(mixed_r, out_full)
    normed2, inv_rms2 = rms_forward(residual, norm_gain2)
    normed2_r = normed2.astype(BF16)
    normed2_f = normed2_r.astype(F32)
    arrived = exchange(dot_nn(hot, normed2_r).astype(BF16))
    logits = jnp.dot(normed2_f, w_router, precision=HIGHEST)
    route_hot = (routes[:, :, None] == expert_ids[None, None, :]).astype(F32)
    chosen = jnp.sum(logits[:, None, :] * route_hot, axis=-1)
    gate_probs = jax.nn.softmax(chosen, axis=-1)
    grad_y = grad_out.astype(F32)
    back0 = (gate_probs[:, 0:1] * grad_y).astype(BF16)
    back1 = (gate_probs[:, 1:2] * grad_y).astype(BF16)
    grad_produced = exchange((dot_nn(hot0, back0) + dot_nn(hot1, back1)).astype(BF16))

    w_in = w_expert_in[0]
    w_out = w_expert_out[0]
    gate_pre = dot_nn(arrived, w_in[0])
    up_pre = dot_nn(arrived, w_in[1])
    gelu_val, gelu_back = jax.vjp(jax.nn.gelu, gate_pre)
    hidden_r = (gelu_val * up_pre).astype(BF16)
    produced = dot_nn(hidden_r, w_out).astype(BF16)
    returned = exchange(produced)
    grad_hidden = dot_nt(grad_produced, w_out)
    grad_gate_r = gelu_back(grad_hidden * up_pre)[0].astype(BF16)
    grad_up_r = (grad_hidden * gelu_val).astype(BF16)
    grad_arrived = (dot_nt(grad_gate_r, w_in[0]) + dot_nt(grad_up_r, w_in[1])).astype(BF16)
    grad_returned = exchange(grad_arrived)
    grad_w_out = dot_nn(hidden_r.T, grad_produced)
    grad_w_in = jnp.stack(
        [dot_nn(arrived.T, grad_gate_r), dot_nn(arrived.T, grad_up_r)], axis=0
    )
    grad_expert_out = lax.psum_scatter(
        grad_w_out[None].astype(BF16), "dp", scatter_dimension=2, tiled=True
    ).astype(F32)
    grad_expert_in = lax.psum_scatter(
        grad_w_in[None].astype(BF16), "dp", scatter_dimension=2, tiled=True
    ).astype(F32)

    first_out = dot_nn(hot0.T, returned)
    second_out = dot_nn(hot1.T, returned)
    block_out = (
        residual + gate_probs[:, 0:1] * first_out + gate_probs[:, 1:2] * second_out
    ).astype(BF16)
    grad_gates = jnp.stack(
        [jnp.sum(grad_y * first_out, axis=-1), jnp.sum(grad_y * second_out, axis=-1)], axis=1
    )
    grad_chosen = gate_probs * (
        grad_gates - jnp.sum(gate_probs * grad_gates, axis=-1, keepdims=True)
    )
    grad_logits = jnp.sum(grad_chosen[:, :, None] * route_hot, axis=1)
    grad_router = jnp.dot(normed2_f.T, grad_logits, precision=HIGHEST)
    grad_normed2 = jnp.dot(grad_logits, w_router.T, precision=HIGHEST) + dot_nn(
        hot.T, grad_returned
    )
    grad_res_norm, grad_gain2 = rms_backward(residual, inv_rms2, norm_gain2, grad_normed2)
    grad_residual = grad_y + grad_res_norm
    grad_attn_r = grad_residual.astype(BF16)
    grad_out_w = dot_nn(mixed_r.T, grad_attn_r)
    grad_mixed_r = dot_nt(grad_attn_r, out_full).astype(BF16)
    grad_q, grad_k, grad_v, folded = attend_back(qkv_r, probs, grad_mixed_r)
    grad_qkv_r = jnp.concatenate([grad_q, grad_k, grad_v], axis=1)
    grad_qkv_w = dot_nn(normed1_r.T, grad_qkv_r)
    grad_normed1 = dot_nt(grad_qkv_r, qkv_full)
    grad_in_norm, grad_gain1 = rms_backward(inputs_f, inv_rms1, norm_gain1, grad_normed1)
    grad_tokens = grad_residual + grad_in_norm
    grad_bias_local = lax.dot_general(
        bucket_hot, folded, (((1,), (1,)), ((), ())), precision=HIGHEST
    )
    grad_bias, grad_norm1, grad_norm2, grad_router_all = lax.psum(
        (grad_bias_local, grad_gain1, grad_gain2, grad_router), ("dp", "expert")
    )
    grad_out_proj = lax.psum_scatter(
        grad_out_w.astype(BF16), ("dp", "expert"), scatter_dimension=0, tiled=True
    ).astype(F32)
    grad_qkv = lax.psum_scatter(
        grad_qkv_w.astype(BF16), ("dp", "expert"), scatter_dimension=0, tiled=True
    ).astype(F32)
    return (
        block_out,
        grad_tokens,
        grad_norm1,
        grad_qkv,
        grad_out_proj,
        grad_bias,
        grad_norm2,
        grad_router_all,
        grad_expert_in,
        grad_expert_out,
    )


def solution(mesh):
    split = P(("dp", "expert"), None)
    in_specs = (
        split,
        split,
        P(),
        P(),
        split,
        split,
        P(),
        P(),
        P(),
        P("expert", None, None, None),
        P("expert", None, None),
        split,
    )
    out_specs = (
        split,
        split,
        P(),
        split,
        split,
        P(),
        P(),
        P(),
        P("expert", None, "dp", None),
        P("expert", None, "dp"),
    )
    return jax.shard_map(shards, mesh=mesh, in_specs=in_specs, out_specs=out_specs, check_vma=False)
```

time: 3010 us -> 973 us (0.32)
  local copies, waits for them, and re-layouts: 2210 us -> 9.04 us
  waiting for transfers between devices: 297 us -> 532 us
  matrix products: 241 us -> 179 us
  other arithmetic: 64.4 us -> 24.4 us
  Pallas kernels: 0 us -> 32 us
    gather x3 -> x0, local copies, waits for them, and re-layouts: 2140 us -> none  [the longest x1 2130 us: shards(): bucket_pos = jnp.take(rel_bucket, distance.reshape(-1))]
    reduce_scatter x4, waiting for transfers between devices: 185 us -> 308 us  [the longest x1 118 us: shards(): lax.psum_scatter(grad_qkv_w.astype(BF16), ('dp', 'expert'), scatter_dimen...]
    all_gather x2, waiting for transfers between devices: 0.04 us -> 104 us  [the longest x1 69.7 us: shards(): qkv_full = lax.all_gather(w_qkv, ('dp', 'expert'), axis=0, tiled=True)]
    dot_general x28 -> x27, matrix products: 241 us -> 179 us  [the longest x17 113 us: dot_nn(): return jnp.dot(a, b, preferred_element_type=F32)]
    unnamed x113 -> x57, local copies, waits for them, and re-layouts: 50.9 us -> 8.96 us
    pallas_call x0 -> x2, Pallas kernels: none -> 32 us  [the longest x1 16.7 us: attend_back(): pl.pallas_call(body, grid=(8,), in_specs=[pair_spec(0), pair_spec(8), pai...]
  transfers between devices with their start and end apart: 8 -> 8, of which waited for: 4 -> 8; matrix products, arithmetic and copies ran while one was open for 80% -> 8% of each run, Pallas kernels for 0% -> 3%
where the time goes in v1:
time: 973 us; the launch traced here: 966 us
  waiting for transfers between devices  532 us (55%)
  matrix products  179 us (18%)
  blocking collectives  166 us (17%)
  Pallas kernels  32 us (3%)
  other arithmetic  24.4 us (3%)
  between operations  14.8 us (2%)
  starting transfers between devices  9.78 us (1%)
    all_to_all x2, blocking collectives, exchange(): lax.all_to_all(rows.reshape(expert_count, capacity, model_width), 'expert...  128 us
    all_to_all x2, waiting for transfers between devices, exchange(): lax.all_to_all(rows.reshape(expert_count, capacity, model_width), 'expert...  118 us
    reduce_scatter x1, waiting for transfers between devices, shards(): lax.psum_scatter(grad_qkv_w.astype(BF16), ('dp', 'expert'), scatter_dimen...  118 us
    reduce_scatter x1, waiting for transfers between devices, shards(): lax.psum_scatter(grad_w_in[None].astype(BF16), 'dp', scatter_dimension=2,...  113 us
    dot_general x17, matrix products, dot_nn(): return jnp.dot(a, b, preferred_element_type=F32)  113 us
    all_gather x1, waiting for transfers between devices, shards(): qkv_full = lax.all_gather(w_qkv, ('dp', 'expert'), axis=0, tiled=True)  69.7 us
    reduce_scatter x1, waiting for transfers between devices, shards(): lax.psum_scatter(grad_w_out[None].astype(BF16), 'dp', scatter_dimension=2...  64.7 us
    dot_general x5, matrix products, dot_nt(): lax.dot_general(a, b, (((1,), (1,)), ((), ())), preferred_element_type=F32)  59.8 us
  transfers between devices with their start and end apart: 8, of which 8 were waited for; matrix products, arithmetic and copies ran while one was open for 8% of the time, Pallas kernels for 3%

profile of v1, /device:TPU:0, one launch (start us, length us, event | category | flops | bytes accessed | tf_op | source)
XLA Modules:
  0.0 966.0 jit_solution(18263286921531372263)
XLA Ops:
  13.6 69.7 %all-gather.3.cloned.1.call-done = bf16[1024,3072]{1,0:T(8,128)(2,1)} async-done(((bf16[32,3072]{1,0:T(8,128)(2,1)}), bf16[1024,3072]{1,0:T(8,128)(2,1)}) %all-gather.3.cloned.1.call-update) | async-done | bytes 6291472 | tf_op jit(solution)/shard_map/all_gather | solution.py:187
  83.3 6.6 convolution_convert_fusion.1.refs_0_.refs_1_.refs_2_
  89.9 15.3 %shard_map.195 = (bf16[512,1024]{1,0:T(8,128)(2,1)S(1)}, bf16[16,512,512]{2,1,0:T(8,128)(2,1)}) custom-call(bf16[512,3072]{1,0:T(8,128)(2,1)S(1)} %convolution_convert_fusion.1.refs_0_.refs_1_.refs_2_, bf16[512,3072]{1,0:T(8,128)(2,1)S(1)} %convolution_convert_fusion.1.refs_0_.refs_1_.refs_2_, ...), custom_call_target="tpu_custom_call" | custom-call | tf_op jit(solution)/shard_map/pallas_call | solution.py:123
  106.8 34.4 %all-gather.5.cloned.1.call-done = bf16[1024,1024]{1,0:T(8,128)(2,1)} async-done(((bf16[32,1024]{1,0:T(8,128)(2,1)}), bf16[1024,1024]{1,0:T(8,128)(2,1)}) %all-gather.5.cloned.1.call-update) | async-done | bytes 2097168 | tf_op jit(solution)/shard_map/all_gather | solution.py:188
  146.5 63.9 %all_to_all.20 = bf16[8,160,1024]{2,1,0:T(8,128)(2,1)S(1)} all-to-all(bf16[8,160,1024]{2,1,0:T(8,128)(2,1)S(1)} %bitcast.87), channel_id=1, replica_groups=mesh['dp'=4,'expert'=8] {'expert'}, dimensions={0} | all-to-all | bytes 5242880 | tf_op jit(solution)/shard_map/all_to_all | solution.py:191
  210.4 10.3 %fusion.17 = f32[1280,2816]{1,0:T(8,128)} fusion(bf16[1280,1024]{1,0:T(8,128)(2,1)S(1)} %bitcast.78, bf16[1,2,1024,2816]{3,2,1,0:T(8,128)(2,1)S(1)} %bitcast.100), kind=kOutput, calls=%fused_computation.23 | convolution fusion | flops 7381975040 | bytes 22806528 | tf_op jit(solution)/shard_map/dot_general | solution.py:22
  220.7 19.1 %multiply_convert_fusion.1 = (bf16[1280,2816]{1,0:T(8,128)(2,1)}, f32[1280,2816]{1,0:T(8,128)}) fusion(f32[1280,2816]{1,0:T(8,128)} %fusion.17, bf16[1280,1024]{1,0:T(8,128)(2,1)S(1)} %bitcast.79, bf16[1,2,1024,2816]{3,2,1,0:T(8,128)(2,1)} %param.21), kind=kOutput, calls=%fused_computation.10 | convolution fusion | flops 7418019840 | bytes 44433408 | tf_op jit(solution)/shard_map/dot_general | solution.py:22
  239.8 12.6 %fusion.26 = bf16[1280,1024]{1,0:T(8,128)(2,1)} fusion(bf16[1280,2816]{1,0:T(8,128)(2,1)} %get-tuple-element.44, bf16[1,2816,1024]{2,1,0:T(8,128)(2,1)} %param.22), kind=kOutput, calls=%fused_computation.43 | convolution fusion | flops 7383285760 | bytes 15597568 | tf_op jit(solution)/shard_map/dot_general | solution.py:22
  252.4 4.8 all-to-all-start.1
  259.4 58.1 %all-to-all-done.1 = bf16[8,160,1024]{2,1,0:T(8,128)(2,1)} async-done(((bf16[8,160,1024]{2,1,0:T(8,128)(2,1)}), bf16[8,160,1024]{2,1,0:T(8,128)(2,1)}, u32[]{:S(2)}, u32[]{:S(2)}) %all-to-all-start.1) | async-done | bytes 2621472 | tf_op jit(solution)/shard_map/all_to_all | solution.py:191
  317.4 3.4 fusion.33
  320.9 5.5 fusion.45
  329.8 63.9 %all_to_all.21 = bf16[8,160,1024]{2,1,0:T(8,128)(2,1)} all-to-all(bf16[8,160,1024]{2,1,0:T(8,128)(2,1)S(1)} %bitcast.86), channel_id=1, replica_groups=mesh['dp'=4,'expert'=8] {'expert'}, dimensions={0} | all-to-all | bytes 5242880 | tf_op jit(solution)/shard_map/all_to_all | solution.py:191
  393.6 25.1 %fusion.6 = (bf16[1280,2816]{1,0:T(8,128)(2,1)}, bf16[1280,2816]{1,0:T(8,128)(2,1)}) fusion(f32[1280,2816]{1,0:T(8,128)} %fusion.17, f32[1280,2816]{1,0:T(8,128)} %get-tuple-element.45, bf16[1280,1024]{1,0:T(8,128)(2,1)} %bitcast.82, bf16[1,2816,1024]{2,1,0:T(8,128)(2,1)} %param.22), kind=kOutput, calls=%fused_computation.8 | convolution fusion | flops 7468482560 | bytes 51642368 | tf_op jit(solution)/shard_map/dot_general | solution.py:18
  418.7 11.7 %fusion.11 = f32[1280,1024]{1,0:T(8,128)S(1)} fusion(bf16[1280,2816]{1,0:T(8,128)(2,1)} %get-tuple-element.35, bf16[1,2,1024,2816]{3,2,1,0:T(8,128)(2,1)} %param.21), kind=kOutput, calls=%fused_computation.17 | convolution fusion | flops 7381975040 | bytes 18219008 | tf_op jit(solution)/shard_map/dot_general | solution.py:18
  430.4 11.1 %add_convert_fusion = bf16[1280,1024]{1,0:T(8,128)(2,1)} fusion(f32[1280,1024]{1,0:T(8,128)S(1)} %fusion.11, bf16[1280,2816]{1,0:T(8,128)(2,1)S(1)} %copy-done.23, bf16[1,2,1024,2816]{3,2,1,0:T(8,128)(2,1)} %param.21), kind=kOutput, calls=%fused_computation.29 | convolution fusion | flops 7384596480 | bytes 20840448 | tf_op jit(solution)/shard_map/dot_general | solution.py:18
  441.5 4.4 all-to-all-start.3
  446.2 60.0 %all-to-all-done.3 = bf16[8,160,1024]{2,1,0:T(8,128)(2,1)} async-done(((bf16[8,160,1024]{2,1,0:T(8,128)(2,1)}), bf16[8,160,1024]{2,1,0:T(8,128)(2,1)}, u32[]{:S(2)}, u32[]{:S(2)}) %all-to-all-start.3) | async-done | bytes 2621472 | tf_op jit(solution)/shard_map/all_to_all | solution.py:191
  518.1 12.3 %convert_bitcast_fusion = bf16[1,2816,1024]{2,1,0:T(8,128)(2,1)} fusion(bf16[1280,2816]{1,0:T(8,128)(2,1)} %get-tuple-element.44, bf16[1280,1024]{1,0:T(8,128)(2,1)} %bitcast.83), kind=kOutput, calls=%fused_computation.25 | convolution fusion | flops 7384858624 | bytes 15597568 | tf_op jit(solution)/shard_map/dot_general | solution.py:22
  534.9 16.7 %shard_map.196 = (bf16[512,1024]{1,0:T(8,128)(2,1)S(1)}, bf16[512,1024]{1,0:T(8,128)(2,1)S(1)}, bf16[512,1024]{1,0:T(8,128)(2,1)S(1)}, f32[16,1024]{1,0:T(8,128)S(1)}) custom-call(bf16[512,3072]{1,0:T(8,128)(2,1)} %copy-done.1, bf16[512,3072]{1,0:T(8,128)(2,1)} %copy-done.1, bf16[512,3072]{1,0:T(8,128)(2,1)} %copy-done.1, ...), custom_call_target="tpu_custom_call" | custom-call | tf_op jit(solution)/shard_map/pallas_call | solution.py:140
  553.6 5.5 convolution_convert_fusion
  559.4 11.5 %convert_bitcast_fusion.2 = bf16[1,1,1024,2816]{3,2,1,0:T(8,128)(2,1)S(1)} fusion(bf16[1280,1024]{1,0:T(8,128)(2,1)} %bitcast.80, bf16[1280,2816]{1,0:T(8,128)(2,1)} %get-tuple-element.34), kind=kOutput, calls=%fused_computation.27 | convolution fusion | flops 7384858624 | bytes 15597568 | tf_op jit(solution)/shard_map/dot_general | solution.py:22
  571.0 11.1 %convert_bitcast_fusion.1 = bf16[1,1,1024,2816]{3,2,1,0:T(8,128)(2,1)S(1)} fusion(bf16[1280,1024]{1,0:T(8,128)(2,1)S(1)} %bitcast.81, bf16[1280,2816]{1,0:T(8,128)(2,1)} %get-tuple-element.35), kind=kOutput, calls=%fused_computation.26 | convolution fusion | flops 7384858624 | bytes 15597568 | tf_op jit(solution)/shard_map/dot_general | solution.py:22
  582.1 5.3 pad_maximum_fusion
  589.3 9.0 fusion.43
  598.3 38.0 %all-reduce.1 = (f32[1024]{0:T(1024)}, f32[32,16]{0,1:T(8,128)}, f32[1024]{0:T(1024)}, f32[1024,8]{0,1:T(8,128)}) all-reduce(f32[1024]{0:T(1024)S(1)} %get-tuple-element.24, f32[32,16]{0,1:T(8,128)S(1)} %fusion.71, f32[1024]{0:T(1024)S(1)} %get-tuple-element.22, ...), channel_id=1, replica_groups=mesh['dp'=4,'expert'=8] {'dp','expert'}, use_global_device_ids=true, to_apply=%region_13.14 | all-reduce | flops 10752 | bytes 86016 | tf_op jit(solution)/shard_map/psum | solution.py:293
  636.3 3.5 fusion.42
  639.8 13.1 %reduce-scatter.7.cloned.1.call-done = bf16[32,1024]{1,0:T(8,128)(2,1)} async-done(((bf16[1024,1024]{1,0:T(8,128)(2,1)}), bf16[32,1024]{1,0:T(8,128)(2,1)}) %reduce-scatter.7.cloned.1.call-update) | async-done | bytes 65552 | tf_op jit(solution)/shard_map/reduce_scatter | solution.py:296
  654.4 64.7 %reduce-scatter.11.cloned.1.call-done = bf16[1,2816,256]{2,1,0:T(8,128)(2,1)} async-done(((bf16[1,2816,1024]{2,1,0:T(8,128)(2,1)}), bf16[1,2816,256]{2,1,0:T(8,128)(2,1)}) %reduce-scatter.11.cloned.1.call-update) | async-done | bytes 1441808 | tf_op jit(solution)/shard_map/reduce_scatter | solution.py:256
  722.2 117.5 %reduce-scatter.5.cloned.1.call-done = bf16[32,3072]{1,0:T(8,128)(2,1)} async-done(((bf16[1024,3072]{1,0:T(8,128)(2,1)}), bf16[32,3072]{1,0:T(8,128)(2,1)}) %reduce-scatter.5.cloned.1.call-update) | async-done | bytes 196624 | tf_op jit(solution)/shard_map/reduce_scatter | solution.py:299
  841.5 112.8 %reduce-scatter.9.cloned.1.call-done = bf16[1,2,256,2816]{3,2,1,0:T(8,128)(2,1)} async-done(((bf16[1,2,1024,2816]{3,2,1,0:T(8,128)(2,1)}), bf16[1,2,256,2816]{3,2,1,0:T(8,128)(2,1)}) %reduce-scatter.9.cloned.1.call-update) | async-done | bytes 2883600 | tf_op jit(solution)/shard_map/reduce_scatter | solution.py:259
  954.2 4.8 convert_element_type.122
  (104 shorter events, 45.6 us)
Async XLA Ops:
  7.2 250.0 %copy-start = (f32[1024,8]{0,1:T(8,128)S(1)}, f32[1024,8]{0,1:T(8,128)}, u32[]{:S(2)}) copy-start(f32[1024,8]{0,1:T(8,128)} %param.20) | copy-start | bytes 98308
  7.2 76.1 %all-gather.3.cloned.1.call-start = ((), (), s32[]{:S(2)}) async-start(), calls=%async_computation.8 | async-start | bytes 6488064 | tf_op jit(solution)/shard_map/all_gather | solution.py:187
  7.9 133.3 %all-gather.5.cloned.1.call-start = ((), (), s32[]{:S(2)}) async-start(), calls=%async_computation.9 | async-start | bytes 2162688 | tf_op jit(solution)/shard_map/all_gather | solution.py:188
  11.4 71.9 %copy-start.20 = (f32[512]{0:T(512)}, f32[512]{0:T(512)S(1)}, u32[]{:S(2)}) copy-start(f32[512]{0:T(512)S(1)} %add_rsqrt_fusion.1) | copy-start | bytes 6148
  105.2 1.6 copy-start.1
  141.3 3.4 copy-start.18
  141.3 69.1 %slice-start = ((s8[11534336]{0:T(1024)(128)(4,1)}), s8[4194304]{0:T(1024)(128)(4,1)S(1)}, s32[]{:S(2)}) async-start(s8[11534336]{0:T(1024)(128)(4,1)} %bitcast.99), calls=%async_computation.14 | async-start | bytes 8388608
  144.7 65.7 %slice-start.1 = ((s8[11534336]{0:T(1024)(128)(4,1)}), s8[4194304]{0:T(1024)(128)(4,1)S(1)}, s32[]{:S(2)}) async-start(s8[11534336]{0:T(1024)(128)(4,1)} %bitcast.99), calls=%async_computation.15 | async-start | bytes 8388608
  144.9 1.6 copy-start.2
  144.9 65.5 %slice-start.2 = ((s8[11534336]{0:T(1024)(128)(4,1)}), s8[3145728]{0:T(1024)(128)(4,1)S(1)}, s32[]{:S(2)}) async-start(s8[11534336]{0:T(1024)(128)(4,1)} %bitcast.99), calls=%async_computation.16 | async-start | bytes 6291456
  210.4 10.3 %copy-start.8 = (bf16[8,160,1024]{2,1,0:T(8,128)(2,1)}, bf16[8,160,1024]{2,1,0:T(8,128)(2,1)S(1)}, u32[]{:S(2)}) copy-start(bf16[8,160,1024]{2,1,0:T(8,128)(2,1)S(1)} %all_to_all.20) | copy-start | bytes 7864324
  252.4 6.9 copy-start.19
  252.4 65.1 %all-to-all-start.1 = ((bf16[8,160,1024]{2,1,0:T(8,128)(2,1)}), bf16[8,160,1024]{2,1,0:T(8,128)(2,1)}, u32[]{:S(2)}, u32[]{:S(2)}) async-start(bf16[8,160,1024]{2,1,0:T(8,128)(2,1)} %bitcast.85), calls=%async_computation.1 | async-start | bytes 5242880 | tf_op jit(solution)/shard_map/all_to_all | solution.py:191
  317.4 3.4 copy-start.13
  320.8 5.5 copy-start.10
  418.7 11.7 %copy-start.23 = (bf16[1280,2816]{1,0:T(8,128)(2,1)S(1)}, bf16[1280,2816]{1,0:T(8,128)(2,1)}, u32[]{:S(2)}) copy-start(bf16[1280,2816]{1,0:T(8,128)(2,1)} %get-tuple-element.34) | copy-start | bytes 21626884
  441.5 64.7 %all-to-all-start.3 = ((bf16[8,160,1024]{2,1,0:T(8,128)(2,1)}), bf16[8,160,1024]{2,1,0:T(8,128)(2,1)}, u32[]{:S(2)}, u32[]{:S(2)}) async-start(bf16[8,160,1024]{2,1,0:T(8,128)(2,1)} %bitcast.84), calls=%async_computation.3 | async-start | bytes 5242880 | tf_op jit(solution)/shard_map/all_to_all | solution.py:191
  445.9 206.9 %reduce-scatter.7.cloned.1.call-start = ((), (), s32[]{:S(2)}) async-start(), calls=%async_computation.11 | async-start | bytes 2162688 | tf_op jit(solution)/shard_map/reduce_scatter | solution.py:296
  509.6 2.6 copy-start.11
  509.6 2.6 copy-start.12
  509.6 2.5 copy-start.14
  518.0 201.0 %reduce-scatter.11.cloned.1.call-start = ((), (), s32[]{:S(2)}) async-start(), calls=%async_computation.13 | async-start | bytes 7208960 | tf_op jit(solution)/shard_map/reduce_scatter | solution.py:256
  530.4 1.6 copy-start.5
  530.4 309.3 %reduce-scatter.5.cloned.1.call-start = ((), (), s32[]{:S(2)}) async-start(), calls=%async_computation.10 | async-start | bytes 6488064 | tf_op jit(solution)/shard_map/reduce_scatter | solution.py:299
  551.7 1.9 copy-start.6
  551.7 1.9 copy-start.21
  551.7 1.9 copy-start.22
  551.9 1.7 copy-start.15
  559.2 395.0 %reduce-scatter.9.cloned.1.call-start = ((), (), s32[]{:S(2)}) async-start(), calls=%async_computation.12 | async-start | bytes 14417920 | tf_op jit(solution)/shard_map/reduce_scatter | solution.py:259
  559.4 11.6 %copy-start.9 = (bf16[8,160,1024]{2,1,0:T(8,128)(2,1)S(1)}, bf16[8,160,1024]{2,1,0:T(8,128)(2,1)}, u32[]{:S(2)}) copy-start(bf16[8,160,1024]{2,1,0:T(8,128)(2,1)} %copy-done.8) | copy-start | bytes 7864324
  587.4 1.7 copy-start.17
  589.3 47.0 %copy-start.7 = (bf16[512,1024]{1,0:T(8,128)(2,1)S(1)}, bf16[512,1024]{1,0:T(8,128)(2,1)}, u32[]{:S(2)}) copy-start(bf16[512,1024]{1,0:T(8,128)(2,1)} %param.12) | copy-start | bytes 3145732
  (3 other events, 3.2 us)
Sparse Core Ops, SparseCore 0:
  11.0 72.1 all-gather.2
  86.2 54.9 all-gather.4
  518.1 134.6 reduce-scatter.6
  656.6 62.4 reduce-scatter.10
  725.5 114.2 reduce-scatter.4
  842.7 111.4 reduce-scatter.8

commit v2 on v1

--- a/solution.py
+++ b/solution.py
@@ -152,6 +152,522 @@
     )(qkv, qkv, qkv, probs, grad_mixed)
 
 
+MESH = pl.DeviceIdType.MESH
+ANY = pl.BlockSpec(memory_space=pl.ANY)
+GROUPS = 4
+TILE = 256
+
+
+def flip(index, mask):
+    bit = 1
+    while bit <= mask:
+        if mask & bit:
+            index = index + bit - 2 * bit * ((index // bit) % 2)
+        bit *= 2
+    return index
+
+
+def remote(src, dst, send_sem, recv_sem, **axes):
+    return pltpu.make_async_remote_copy(
+        src_ref=src,
+        dst_ref=dst,
+        send_sem=send_sem,
+        recv_sem=recv_sem,
+        device_id=axes,
+        device_id_type=MESH,
+    )
+
+
+def greet(partners):
+    barrier = pltpu.get_barrier_semaphore()
+    for axes in partners:
+        pl.semaphore_signal(barrier, inc=1, device_id=axes, device_id_type=MESH)
+    pl.semaphore_wait(barrier, len(partners))
+
+
+def gelu_parts(x):
+    root = 0.7978845608028654
+    square = x * x
+    t = jnp.tanh(root * x * (1.0 + 0.044715 * square))
+    half = 0.5 * (1.0 + t)
+    slope = half + 0.5 * x * (1.0 - t * t) * (root * (1.0 + 3 * 0.044715 * square))
+    return x * half, slope
+
+
+def experts_kernel(
+    xs_ref,
+    dys_ref,
+    w_in_ref,
+    w_out_ref,
+    y_back_ref,
+    dx_back_ref,
+    dw_ref,
+    w_in_v,
+    w_out_v,
+    x_v,
+    dy_v,
+    hid_v,
+    dgate_v,
+    dup_v,
+    y_v,
+    dx_v,
+    y_sum,
+    dx_sum,
+    stage,
+    local_sem,
+    stage_sem,
+    x_send,
+    x_recv,
+    dy_send,
+    dy_recv,
+    y_send,
+    y_recv,
+    dx_send,
+    dx_recv,
+):
+    expert_count, capacity, width = xs_ref.shape
+    hidden = w_out_ref.shape[0]
+    tiles = hidden // TILE
+    size = expert_count // GROUPS
+    rows = size * capacity
+    me = lax.axis_index("expert")
+    my_group, my_place = me // size, me % size
+
+    def others(c):
+        group = flip(my_group, c)
+        return [group * size + (my_place + s) % size for s in range(1 if c == 0 else 0, size)]
+
+    greet([{"expert": (me + d) % expert_count} for d in range(1, expert_count)])
+    for c in (2, 3, 1, 0):
+        for peer in others(c):
+            remote(
+                xs_ref.at[peer], x_v.at[me], x_send.at[peer], x_recv.at[me], expert=peer
+            ).start()
+            remote(
+                dys_ref.at[peer], dy_v.at[me], dy_send.at[peer], dy_recv.at[me], expert=peer
+            ).start()
+    own = [
+        pltpu.make_async_copy(xs_ref.at[me], x_v.at[me], local_sem.at[0]),
+        pltpu.make_async_copy(dys_ref.at[me], dy_v.at[me], local_sem.at[1]),
+        pltpu.make_async_copy(w_in_ref, w_in_v, local_sem.at[2]),
+        pltpu.make_async_copy(w_out_ref, w_out_v, local_sem.at[3]),
+    ]
+    for copy in own:
+        copy.start()
+    for copy in own:
+        copy.wait()
+
+    for c in range(GROUPS):
+        group = flip(my_group, c)
+        span = pl.ds(group * size, size)
+        for peer in others(c):
+            remote(
+                xs_ref.at[peer], x_v.at[peer], x_send.at[peer], x_recv.at[peer], expert=peer
+            ).wait_recv()
+            remote(
+                dys_ref.at[peer], dy_v.at[peer], dy_send.at[peer], dy_recv.at[peer], expert=peer
+            ).wait_recv()
+        y_sum[...] = jnp.zeros_like(y_sum)
+        dx_sum[...] = jnp.zeros_like(dx_sum)
+
+        def step(f, carry, group=group, span=span):
+            cols = pl.ds(pl.multiple_of(f * TILE, TILE), TILE)
+            x = x_v[span].reshape(rows, width)
+            dy = dy_v[span].reshape(rows, width)
+            w_gate, w_up, w_down = w_in_v[0, :, cols], w_in_v[1, :, cols], w_out_v[cols, :]
+            gate, up, dhid = dot_nn(x, w_gate), dot_nn(x, w_up), dot_nt(dy, w_down)
+            gelu, slope = gelu_parts(gate)
+            hid = (gelu * up).astype(BF16)
+            dgate = (dhid * up * slope).astype(BF16)
+            dup = (dhid * gelu).astype(BF16)
+            hid_v[group, :, cols] = hid
+            dgate_v[group, :, cols] = dgate
+            dup_v[group, :, cols] = dup
+            y_sum[...] += dot_nn(hid, w_down)
+            dx_sum[...] += dot_nt(dgate, w_gate) + dot_nt(dup, w_up)
+            return carry
+
+        lax.fori_loop(0, tiles, step, 0)
+        y_v[span] = y_sum[...].astype(BF16).reshape(size, capacity, width)
+        dx_v[span] = dx_sum[...].astype(BF16).reshape(size, capacity, width)
+        for peer in others(c):
+            remote(
+                dx_v.at[peer], dx_back_ref.at[me], dx_send.at[peer], dx_recv.at[me], expert=peer
+            ).start()
+    own = [
+        pltpu.make_async_copy(dx_v.at[me], dx_back_ref.at[me], local_sem.at[0]),
+        pltpu.make_async_copy(y_v.at[me], y_back_ref.at[me], local_sem.at[1]),
+    ]
+    for copy in own:
+        copy.start()
+    for c in (2, 3, 1, 0):
+        for peer in others(c):
+            remote(
+                y_v.at[peer], y_back_ref.at[me], y_send.at[peer], y_recv.at[me], expert=peer
+            ).start()
+
+    slots = expert_count * capacity
+    w_in_v[0, :, 0:slots] = x_v[...].reshape(slots, width).T
+    w_in_v[1, :, 0:slots] = dy_v[...].reshape(slots, width).T
+
+    def put(m, f):
+        return pltpu.make_async_copy(stage.at[m], dw_ref.at[m * tiles + f], stage_sem.at[m])
+
+    def grads(f, carry):
+        cols = pl.ds(pl.multiple_of(f * TILE, TILE), TILE)
+        for m, (side, right) in enumerate(((0, dgate_v), (0, dup_v), (1, hid_v))):
+
+            @pl.when(f > 0)
+            def _():
+                put(m, f - 1).wait()
+
+            block = dot_nn(w_in_v[side, :, 0:slots], right[:, :, cols].reshape(slots, TILE))
+            stage[m] = block.astype(BF16).reshape(stage.shape[1:])
+            put(m, f).start()
+        return carry
+
+    lax.fori_loop(0, tiles, grads, 0)
+    for m in range(3):
+        put(m, tiles - 1).wait()
+    for copy in own:
+        copy.wait()
+    for c in range(GROUPS):
+        for peer in others(c):
+            for src, dst, send_sem, recv_sem in (
+                (xs_ref, x_v, x_send, x_recv),
+                (dys_ref, dy_v, dy_send, dy_recv),
+            ):
+                remote(
+                    src.at[peer], dst.at[me], send_sem.at[peer], recv_sem.at[me], expert=peer
+                ).wait_send()
+            for src, dst, send_sem, recv_sem in (
+                (dx_v, dx_back_ref, dx_send, dx_recv),
+                (y_v, y_back_ref, y_send, y_recv),
+            ):
+                remote(
+                    src.at[peer], dst.at[me], send_sem.at[peer], recv_sem.at[me], expert=peer
+                ).wait_send()
+                remote(
+                    src.at[peer], dst.at[peer], send_sem.at[peer], recv_sem.at[peer], expert=peer
+                ).wait_recv()
+
+
+def experts(xs, dys, w_in, w_out, dp_count):
+    expert_count, capacity, width = xs.shape
+    hidden = w_out.shape[0]
+    size = expert_count // GROUPS
+    tiles = hidden // TILE
+    rows = size * capacity
+    slots = jax.ShapeDtypeStruct(xs.shape, BF16)
+    parts = (dp_count, width // dp_count, TILE)
+    peers = pltpu.SemaphoreType.DMA((expert_count,))
+    return pl.pallas_call(
+        experts_kernel,
+        in_specs=[ANY] * 4,
+        out_specs=[ANY] * 3,
+        out_shape=[slots, slots, jax.ShapeDtypeStruct((3 * tiles, *parts), BF16)],
+        scratch_shapes=[
+            pltpu.VMEM(w_in.shape, BF16),
+            pltpu.VMEM(w_out.shape, BF16),
+            pltpu.VMEM(xs.shape, BF16),
+            pltpu.VMEM(xs.shape, BF16),
+            pltpu.VMEM((GROUPS, rows, hidden), BF16),
+            pltpu.VMEM((GROUPS, rows, hidden), BF16),
+            pltpu.VMEM((GROUPS, rows, hidden), BF16),
+            pltpu.VMEM(xs.shape, BF16),
+            pltpu.VMEM(xs.shape, BF16),
+            pltpu.VMEM((rows, width), F32),
+            pltpu.VMEM((rows, width), F32),
+            pltpu.VMEM((3, *parts), BF16),
+            pltpu.SemaphoreType.DMA((4,)),
+            pltpu.SemaphoreType.DMA((3,)),
+        ]
+        + [peers] * 8,
+        compiler_params=pltpu.CompilerParams(
+            collective_id=1, has_side_effects=True, vmem_limit_bytes=61 * 1024 * 1024
+        ),
+        name="experts",
+    )(xs, dys, w_in, w_out)
+
+
+def reduce_kernel(part_count, *refs):
+    dw_ref, small_ref = refs[:2]
+    parts_in = refs[2 : 2 + part_count]
+    refs = refs[2 + part_count :]
+    g_in_ref, g_out_ref, small_out_ref = refs[:3]
+    parts_out = refs[3 : 3 + part_count]
+    (
+        own_v,
+        first_v,
+        second_v,
+        small_v,
+        part_v,
+        core_v,
+        step1_v,
+        step2_v,
+        last_v,
+        own_sem,
+        first_send,
+        first_recv,
+        second_send,
+        second_recv,
+        small_send,
+        small_recv,
+        part_sem,
+        core_send,
+        core_recv,
+        step1_send,
+        step1_recv,
+        step2_send,
+        step2_recv,
+        last_send,
+        last_recv,
+    ) = refs[3 + part_count :]
+    expert_count = lax.axis_size("expert")
+    chips = expert_count // 2
+    me, dp = lax.axis_index("expert"), lax.axis_index("dp")
+    core, chip = me % 2, me // 2
+    x, y = dp % 2, dp // 2
+    core_peer = me + 1 - 2 * core
+    x_peer, y_peer = dp + 1 - 2 * x, dp + 2 - 4 * y
+    chip_peers = [(chip + d) % chips for d in range(1, chips)]
+    greet(
+        [{"expert": core_peer}, {"dp": x_peer}, {"dp": y_peer}]
+        + [{"expert": peer * 2 + core} for peer in chip_peers]
+    )
+
+    tile_count = dw_ref.shape[0]
+
+    def way(t):
+        q = t % 2
+        sent = [(1 - q) * (2 * i + 1 - x) + q * (2 * (1 - y) + i) for i in range(2)]
+        held = [(1 - q) * (2 * i + x) + q * (2 * y + i) for i in range(2)]
+        peer1 = (1 - q) * x_peer + q * y_peer
+        peer2 = (1 - q) * y_peer + q * x_peer
+        keep = (1 - q) * y + q * x
+        return sent, held, peer1, peer2, keep
+
+    def first_copy(t, i, sent, peer):
+        return remote(
+            dw_ref.at[t, sent[i]], first_v.at[t, i], first_send.at[t, i], first_recv.at[t, i], dp=peer
+        )
+
+    def own_copy(t, i, held):
+        return pltpu.make_async_copy(dw_ref.at[t, held[i]], own_v.at[t, i], own_sem.at[t, i])
+
+    def second_copy(t, keep, peer):
+        return remote(own_v.at[t, 1 - keep], second_v.at[t], second_send.at[t], second_recv.at[t], dp=peer)
+
+    def begin(t, carry):
+        sent, held, peer1, _, _ = way(t)
+        for i in range(2):
+            first_copy(t, i, sent, peer1).start()
+        for i in range(2):
+            own_copy(t, i, held).start()
+        return carry
+
+    def relay(t, carry):
+        sent, held, peer1, peer2, keep = way(t)
+        for i in range(2):
+            own_copy(t, i, held).wait()
+            first_copy(t, i, sent, peer1).wait_recv()
+        pass_on = own_v[t, 1 - keep].astype(F32) + first_v[t, 1 - keep].astype(F32)
+        own_v[t, 1 - keep] = pass_on.astype(BF16)
+        second_copy(t, keep, peer2).start()
+        return carry
+
+    def finish(m, out_ref):
+        tiles = tile_count // 3
+
+        def body(f, carry):
+            t = m * tiles + f
+            sent, held, peer1, peer2, keep = way(t)
+            second_copy(t, keep, peer2).wait()
+            for i in range(2):
+                first_copy(t, i, sent, peer1).wait_send()
+            total = own_v[t, keep].astype(F32) + first_v[t, keep].astype(F32)
+            cols = pl.ds(pl.multiple_of(f * TILE, TILE), TILE)
+            out_ref[:, cols] = total + second_v[t].astype(F32)
+            return carry
+
+        lax.fori_loop(0, tiles, body, 0)
+
+    half = parts_in[0].shape[-1] // 2
+
+    def part_core(p):
+        return remote(
+            parts_in[p].at[:, :, :, 1 - core], core_v.at[p], core_send.at[p], core_recv.at[p], expert=core_peer
+        )
+
+    def part_own(p):
+        return pltpu.make_async_copy(parts_in[p].at[:, :, :, core], part_v.at[p], part_sem.at[p])
+
+    def part_step1(p, b):
+        src = (
+            part_v.at[p, :, 1 - x, :, :, 0:half]
+            if b == 0
+            else part_v.at[p, 1 - y, :, :, :, half : 2 * half]
+        )
+        return remote(
+            src, step1_v.at[p, b], step1_send.at[p, b], step1_recv.at[p, b], dp=(x_peer, y_peer)[b]
+        )
+
+    def part_step2(p, b):
+        src = step1_v.at[p, b, (1 - y, 1 - x)[b]]
+        return remote(
+            src, step2_v.at[p, b], step2_send.at[p, b], step2_recv.at[p, b], dp=(y_peer, x_peer)[b]
+        )
+
+    def part_last(p, peer):
+        return remote(
+            part_v.at[p, 0, 0, peer],
+            last_v.at[p, chip],
+            last_send.at[p, peer],
+            last_recv.at[p, chip],
+            expert=peer * 2 + core,
+        )
+
+    def part_arrival(p, peer):
+        return remote(
+            part_v.at[p, 0, 0, peer],
+            last_v.at[p, peer],
+            last_send.at[p, peer],
+            last_recv.at[p, peer],
+            expert=peer * 2 + core,
+        )
+
+    def part_a(p):
+        part_core(p).start()
+        part_own(p).start()
+
+    def part_b(p):
+        part_own(p).wait()
+        part_core(p).wait()
+        part_v[p] = (part_v[p].astype(F32) + core_v[p].astype(F32)).astype(BF16)
+        for b in range(2):
+            part_step1(p, b).start()
+
+    def part_held(p, b, i):
+        return part_v[p, i, x, :, :, 0:half] if b == 0 else part_v[p, y, i, :, :, half : 2 * half]
+
+    def part_c(p):
+        for b in range(2):
+            part_step1(p, b).wait()
+            for i in range(2):
+                total = part_held(p, b, i).astype(F32) + step1_v[p, b, i].astype(F32)
+                step1_v[p, b, i] = total.astype(BF16)
+            part_step2(p, b).start()
+
+    def part_d(p):
+        for b in range(2):
+            part_step2(p, b).wait()
+            total = step1_v[p, b, (y, x)[b]].astype(F32) + step2_v[p, b].astype(F32)
+            part_v[p, 0, 0, :, :, b * half : b * half + half] = total.astype(BF16)
+        for peer in chip_peers:
+            part_last(p, peer).start()
+
+    def part_e(p):
+        total = part_v[p, 0, 0, chip].astype(F32)
+        for peer in chip_peers:
+            part_arrival(p, peer).wait_recv()
+            total = total + last_v[p, peer].astype(F32)
+        parts_out[p][...] = total
+        for peer in chip_peers:
+            part_last(p, peer).wait_send()
+
+    bits = []
+    bit = 1
+    while bit < expert_count:
+        bits.append({"expert": flip(me, bit)})
+        bit *= 2
+    bits += [{"dp": x_peer}, {"dp": y_peer}]
+
+    def small_stage(s):
+        src = small_v.at[s]
+        copy = remote(
+            src, small_v.at[len(bits) + 1 + s], small_send.at[s], small_recv.at[s], **bits[s]
+        )
+        copy.start()
+        copy.wait()
+        small_v[s + 1] = small_v[s] + small_v[len(bits) + 1 + s]
+
+    for p in range(part_count):
+        part_a(p)
+    lax.fori_loop(0, tile_count, begin, 0)
+    small_v[0] = small_ref[...]
+    for p in range(part_count):
+        part_b(p)
+    for s in range(len(bits)):
+        small_stage(s)
+    small_out_ref[...] = small_v[len(bits)]
+    lax.fori_loop(0, tile_count // 2, relay, 0)
+    for p in range(part_count):
+        part_c(p)
+    lax.fori_loop(tile_count // 2, tile_count, relay, 0)
+    for p in range(part_count):
+        part_d(p)
+    for m in range(2):
+        finish(m, g_in_ref.at[m])
+    for p in range(part_count):
+        part_e(p)
+    finish(2, g_out_ref)
+
+
+def reduce_all(dw, small, parts):
+    count = len(parts)
+    tile_count, dp_count, deep, _ = dw.shape
+    expert_count = lax.axis_size("expert")
+    chips = expert_count // 2
+    rows, cols = parts[0].shape
+    own = rows // (dp_count * expert_count)
+    parts = [p.reshape(2, 2, chips, 2, own, cols) for p in parts]
+    bits = expert_count.bit_length() + 1
+    vmem = pl.BlockSpec(memory_space=pltpu.VMEM)
+    sem = pltpu.SemaphoreType.DMA
+    return pl.pallas_call(
+        functools.partial(reduce_kernel, count),
+        in_specs=[ANY, vmem] + [ANY] * count,
+        out_specs=[vmem] * (3 + count),
+        out_shape=[
+            jax.ShapeDtypeStruct((2, deep, tile_count // 3 * TILE), F32),
+            jax.ShapeDtypeStruct((deep, tile_count // 3 * TILE), F32),
+            jax.ShapeDtypeStruct(small.shape, F32),
+        ]
+        + [jax.ShapeDtypeStruct((own, cols), F32)] * count,
+        scratch_shapes=[
+            pltpu.VMEM((tile_count, 2, deep, TILE), BF16),
+            pltpu.VMEM((tile_count, 2, deep, TILE), BF16),
+            pltpu.VMEM((tile_count, deep, TILE), BF16),
+            pltpu.VMEM((2 * bits + 1, *small.shape), F32),
+            pltpu.VMEM((count, 2, 2, chips, own, cols), BF16),
+            pltpu.VMEM((count, 2, 2, chips, own, cols), BF16),
+            pltpu.VMEM((count, 2, 2, chips, own, cols // 2), BF16),
+            pltpu.VMEM((count, 2, chips, own, cols // 2), BF16),
+            pltpu.VMEM((count, chips, own, cols), BF16),
+            sem((tile_count, 2)),
+            sem((tile_count, 2)),
+            sem((tile_count, 2)),
+            sem((tile_count,)),
+            sem((tile_count,)),
+            sem((bits,)),
+            sem((bits,)),
+            sem((count,)),
+            sem((count,)),
+            sem((count,)),
+            sem((count, 2)),
+            sem((count, 2)),
+            sem((count, 2)),
+            sem((count, 2)),
+            sem((count, chips)),
+            sem((count, chips)),
+        ],
+        compiler_params=pltpu.CompilerParams(
+            collective_id=2, has_side_effects=True, vmem_limit_bytes=60 * 1024 * 1024
+        ),
+        name="reduce",
+    )(dw, small, *parts)
+
+
 def rms_forward(values, norm_gain):
     inv_rms = lax.rsqrt(jnp.mean(values * values, axis=-1, keepdims=True) + EPS)
     return (values * inv_rms * norm_gain, inv_rms)
@@ -187,15 +703,6 @@
     qkv_full = lax.all_gather(w_qkv, ("dp", "expert"), axis=0, tiled=True)
     out_full = lax.all_gather(w_out_proj, ("dp", "expert"), axis=0, tiled=True)
 
-    def exchange(rows):
-        return lax.all_to_all(
-            rows.reshape(expert_count, capacity, model_width),
-            "expert",
-            split_axis=0,
-            concat_axis=0,
-            tiled=True,
-        ).reshape(slot_total, model_width)
-
     expert_ids = jnp.arange(expert_count, dtype=jnp.int32)
     pair_expert = routes.T.reshape(2 * row_count)
     pair_hot = pair_expert[:, None] == expert_ids[None, :]
@@ -226,7 +733,7 @@
     normed2, inv_rms2 = rms_forward(residual, norm_gain2)
     normed2_r = normed2.astype(BF16)
     normed2_f = normed2_r.astype(F32)
-    arrived = exchange(dot_nn(hot, normed2_r).astype(BF16))
+    outgoing = dot_nn(hot, normed2_r).astype(BF16)
     logits = jnp.dot(normed2_f, w_router, precision=HIGHEST)
     route_hot = (routes[:, :, None] == expert_ids[None, None, :]).astype(F32)
     chosen = jnp.sum(logits[:, None, :] * route_hot, axis=-1)
@@ -234,32 +741,17 @@
     grad_y = grad_out.astype(F32)
     back0 = (gate_probs[:, 0:1] * grad_y).astype(BF16)
     back1 = (gate_probs[:, 1:2] * grad_y).astype(BF16)
-    grad_produced = exchange((dot_nn(hot0, back0) + dot_nn(hot1, back1)).astype(BF16))
-
-    w_in = w_expert_in[0]
-    w_out = w_expert_out[0]
-    gate_pre = dot_nn(arrived, w_in[0])
-    up_pre = dot_nn(arrived, w_in[1])
-    gelu_val, gelu_back = jax.vjp(jax.nn.gelu, gate_pre)
-    hidden_r = (gelu_val * up_pre).astype(BF16)
-    produced = dot_nn(hidden_r, w_out).astype(BF16)
-    returned = exchange(produced)
-    grad_hidden = dot_nt(grad_produced, w_out)
-    grad_gate_r = gelu_back(grad_hidden * up_pre)[0].astype(BF16)
-    grad_up_r = (grad_hidden * gelu_val).astype(BF16)
-    grad_arrived = (dot_nt(grad_gate_r, w_in[0]) + dot_nt(grad_up_r, w_in[1])).astype(BF16)
-    grad_returned = exchange(grad_arrived)
-    grad_w_out = dot_nn(hidden_r.T, grad_produced)
-    grad_w_in = jnp.stack(
-        [dot_nn(arrived.T, grad_gate_r), dot_nn(arrived.T, grad_up_r)], axis=0
-    )
-    grad_expert_out = lax.psum_scatter(
-        grad_w_out[None].astype(BF16), "dp", scatter_dimension=2, tiled=True
-    ).astype(F32)
-    grad_expert_in = lax.psum_scatter(
-        grad_w_in[None].astype(BF16), "dp", scatter_dimension=2, tiled=True
-    ).astype(F32)
-
+    back_slots = (dot_nn(hot0, back0) + dot_nn(hot1, back1)).astype(BF16)
+    slot_shape = (expert_count, capacity, model_width)
+    returned, grad_returned, grad_w = experts(
+        outgoing.reshape(slot_shape),
+        back_slots.reshape(slot_shape),
+        w_expert_in[0],
+        w_expert_out[0],
+        lax.axis_size("dp"),
+    )
+    returned = returned.reshape(slot_total, model_width)
+    grad_returned = grad_returned.reshape(slot_total, model_width)
     first_out = dot_nn(hot0.T, returned)
     second_out = dot_nn(hot1.T, returned)
     block_out = (
@@ -279,26 +771,42 @@
     grad_res_norm, grad_gain2 = rms_backward(residual, inv_rms2, norm_gain2, grad_normed2)
     grad_residual = grad_y + grad_res_norm
     grad_attn_r = grad_residual.astype(BF16)
-    grad_out_w = dot_nn(mixed_r.T, grad_attn_r)
     grad_mixed_r = dot_nt(grad_attn_r, out_full).astype(BF16)
     grad_q, grad_k, grad_v, folded = attend_back(qkv_r, probs, grad_mixed_r)
     grad_qkv_r = jnp.concatenate([grad_q, grad_k, grad_v], axis=1)
-    grad_qkv_w = dot_nn(normed1_r.T, grad_qkv_r)
     grad_normed1 = dot_nt(grad_qkv_r, qkv_full)
     grad_in_norm, grad_gain1 = rms_backward(inputs_f, inv_rms1, norm_gain1, grad_normed1)
     grad_tokens = grad_residual + grad_in_norm
     grad_bias_local = lax.dot_general(
         bucket_hot, folded, (((1,), (1,)), ((), ())), precision=HIGHEST
     )
-    grad_bias, grad_norm1, grad_norm2, grad_router_all = lax.psum(
-        (grad_bias_local, grad_gain1, grad_gain2, grad_router), ("dp", "expert")
-    )
-    grad_out_proj = lax.psum_scatter(
-        grad_out_w.astype(BF16), ("dp", "expert"), scatter_dimension=0, tiled=True
-    ).astype(F32)
-    grad_qkv = lax.psum_scatter(
-        grad_qkv_w.astype(BF16), ("dp", "expert"), scatter_dimension=0, tiled=True
-    ).astype(F32)
+    small = jnp.concatenate(
+        [
+            grad_router.T,
+            grad_gain1[None],
+            grad_gain2[None],
+            jnp.pad(grad_bias_local.reshape(1, -1), ((0, 0), (0, model_width - bucket_count * head_count))),
+        ],
+        axis=0,
+    )
+    small = jnp.pad(small, ((0, -small.shape[0] % 8), (0, 0)))
+    parts = [
+        dot_nn(left.T, right).astype(BF16)
+        for left, right in (
+            (mixed_r, grad_attn_r),
+            (normed1_r, grad_q),
+            (normed1_r, grad_k),
+            (normed1_r, grad_v),
+        )
+    ]
+    grad_in, grad_out_t, small, grad_out_proj, *grad_qkv = reduce_all(grad_w, small, parts)
+    grad_expert_in, grad_expert_out = grad_in[None], grad_out_t.T[None]
+    grad_qkv = jnp.concatenate(grad_qkv, axis=1)
+    grad_router_all = small[:expert_count].T
+    grad_norm1, grad_norm2 = small[expert_count], small[expert_count + 1]
+    grad_bias = small[expert_count + 2, : bucket_count * head_count].reshape(
+        bucket_count, head_count
+    )
     return (
         block_out,
         grad_tokens,

time: 973 us -> 665 us (0.68)
  Pallas kernels: 32 us -> 460 us
  waiting for transfers between devices: 532 us -> 107 us
  blocking collectives: 166 us -> 0 us
  matrix products: 179 us -> 48.6 us
  other arithmetic: 24.4 us -> 6.79 us
    pallas_call x0 -> x2, Pallas kernels: none -> 428 us  [the longest x1 220 us: experts(): pl.pallas_call(experts_kernel, in_specs=[ANY] * 4, out_specs=[ANY] * 3, o...]
    reduce_scatter x4 -> x0, waiting for transfers between devices: 308 us -> none  [the longest x1 118 us: shards(): lax.psum_scatter(grad_qkv_w.astype(BF16), ('dp', 'expert'), scatter_dimen...]
    all_to_all x2 -> x0, blocking collectives: 128 us -> none  [exchange(): lax.all_to_all(rows.reshape(expert_count, capacity, model_width), 'expert...]
    all_to_all x2 -> x0, waiting for transfers between devices: 118 us -> none  [exchange(): lax.all_to_all(rows.reshape(expert_count, capacity, model_width), 'expert...]
    dot_general x17 -> x13, matrix products: 113 us -> 38 us  [dot_nn(): return jnp.dot(a, b, preferred_element_type=F32)]
    dot_general x5 -> x2, matrix products: 59.8 us -> 6.4 us  [dot_nt(): lax.dot_general(a, b, (((1,), (1,)), ((), ())), preferred_element_type=F32)]
    psum x1 -> x0, blocking collectives: 38 us -> none  [shards(): lax.psum((grad_bias_local, grad_gain1, grad_gain2, grad_router), ('dp', '...]
    convert_element_type x4 -> x0, other arithmetic: 11.1 us -> none  [the longest x1 4.75 us: shards(): grad_expert_in = lax.psum_scatter(grad_w_in[None].astype(BF16), 'dp', sca...]
  transfers between devices with their start and end apart: 8 -> 2, of which waited for: 8 -> 2; matrix products, arithmetic and copies ran while one was open for 8% -> 1% of each run, Pallas kernels for 3% -> 2%
where the time goes in v2:
time: 665 us; the launch traced here: 655 us
  Pallas kernels  460 us (69%)
  waiting for transfers between devices  107 us (16%)
  matrix products  48.6 us (7%)
  local copies, waits for them, and re-layouts  17.6 us (3%)
  between operations  14.6 us (2%)
  other arithmetic  6.79 us (1%)
    pallas_call x1, Pallas kernels, experts(): pl.pallas_call(experts_kernel, in_specs=[ANY] * 4, out_specs=[ANY] * 3, o...  220 us
    pallas_call x1, Pallas kernels, reduce_all(): pl.pallas_call(functools.partial(reduce_kernel, count), in_specs=[ANY, vm...  208 us
    all_gather x1, waiting for transfers between devices, shards(): qkv_full = lax.all_gather(w_qkv, ('dp', 'expert'), axis=0, tiled=True)  71.6 us
    dot_general x13, matrix products, dot_nn(): return jnp.dot(a, b, preferred_element_type=F32)  38 us
    all_gather x1, waiting for transfers between devices, shards(): out_full = lax.all_gather(w_out_proj, ('dp', 'expert'), axis=0, tiled=True)  34.4 us
    pallas_call x1, Pallas kernels, attend_back(): pl.pallas_call(body, grid=(8,), in_specs=[pair_spec(0), pair_spec(8), pai...  16.9 us
    pallas_call x1, Pallas kernels, attend(): pl.pallas_call(body, grid=(8,), in_specs=[pair_spec(0), pair_spec(8), pai...  15.4 us
  transfers between devices with their start and end apart: 2, of which 2 were waited for; matrix products, arithmetic and copies ran while one was open for 1% of the time, Pallas kernels for 2%

profile of v2, /device:TPU:0, one launch (start us, length us, event | category | flops | bytes accessed | tf_op | source)
XLA Modules:
  0.0 655.5 jit_solution(16104392428258264579)
XLA Ops:
  8.0 0.7 all-gather.5.cloned.1.call-update
  9.9 1.5 fusion.22
  11.7 71.6 %all-gather.3.cloned.1.call-done = bf16[1024,3072]{1,0:T(8,128)(2,1)} async-done(((bf16[32,3072]{1,0:T(8,128)(2,1)}), bf16[1024,3072]{1,0:T(8,128)(2,1)}) %all-gather.3.cloned.1.call-update) | async-done | bytes 6291472 | tf_op jit(solution)/shard_map/all_gather | solution.py:703
  83.2 6.6 %convolution_convert_fusion.refs_0_.refs_1_.refs_2_ = bf16[512,3072]{1,0:T(8,128)(2,1)S(1)} fusion(bf16[1024,3072]{1,0:T(8,128)(2,1)} %all-gather.3.cloned.1.call-done, bf16[512,1024]{1,0:T(8,128)(2,1)S(1)} %copy-done.7, f32[1024]{0:T(1024)S(1)} %copy-done.19, f32[512]{0:T(512)S(1)} %add_rsqrt_fusion.1), kind=kOutput, calls=%fused_computation.1 | convolution fusion | flops 3224895488 | bytes 10491904 | tf_op jit(solution)/shard_map/dot_general | solution.py:22
  89.8 15.4 %shard_map.195 = (bf16[512,1024]{1,0:T(8,128)(2,1)S(1)}, bf16[16,512,512]{2,1,0:T(8,128)(2,1)}) custom-call(bf16[512,3072]{1,0:T(8,128)(2,1)S(1)} %convolution_convert_fusion.refs_0_.refs_1_.refs_2_, bf16[512,3072]{1,0:T(8,128)(2,1)S(1)} %convolution_convert_fusion.refs_0_.refs_1_.refs_2_, ...), custom_call_target="tpu_custom_call" | custom-call | tf_op jit(solution)/shard_map/pallas_call | solution.py:123
  105.2 1.7 copy-done.2
  106.9 34.4 %all-gather.5.cloned.1.call-done = bf16[1024,1024]{1,0:T(8,128)(2,1)} async-done(((bf16[32,1024]{1,0:T(8,128)(2,1)}), bf16[1024,1024]{1,0:T(8,128)(2,1)}) %all-gather.5.cloned.1.call-update) | async-done | bytes 2097168 | tf_op jit(solution)/shard_map/all_gather | solution.py:704
  141.2 3.0 multiply_reduce_fusion.2
  144.5 0.9 fusion.63
  145.6 3.1 convolution_convert_fusion.1
  148.7 1.6 fusion.14
  150.3 3.1 add_convert_fusion
  153.5 219.7 %experts.1 = (bf16[8,160,1024]{2,1,0:T(8,128)(2,1)}, bf16[8,160,1024]{2,1,0:T(8,128)(2,1)}, bf16[33,4,256,256]{3,2,1,0:T(8,128)(2,1)}) custom-call(bf16[8,160,1024]{2,1,0:T(8,128)(2,1)} %bitcast.54, bf16[8,160,1024]{2,1,0:T(8,128)(2,1)} %bitcast.55, bf16[2,1024,2816]{2,1,0:T(8,128)(2,1)} %bitcast.50, bf16[2816,1024]{1,0:T(8,128)(2,1)} %bitcast.52), custom_call_target="tpu_custom_call" | custom-call | tf_op jit(solution)/shard_map/experts/pallas_call | solution.py:364
  373.2 3.5 fusion.28
  376.7 1.6 fusion.11
  378.5 3.0 fusion.25
  382.1 2.5 multiply_reduce_fusion
  385.2 2.6 convolution_convert_fusion.5
  387.9 1.3 convolution_convert_fusion.6.refs_4_
  389.2 16.9 %shard_map.196 = (bf16[512,1024]{1,0:T(8,128)(2,1)S(1)}, bf16[512,1024]{1,0:T(8,128)(2,1)S(1)}, bf16[512,1024]{1,0:T(8,128)(2,1)S(1)}, f32[16,1024]{1,0:T(8,128)S(1)}) custom-call(bf16[512,3072]{1,0:T(8,128)(2,1)} %copy-done.2, bf16[512,3072]{1,0:T(8,128)(2,1)} %copy-done.2, bf16[512,3072]{1,0:T(8,128)(2,1)} %copy-done.2, ...), custom_call_target="tpu_custom_call" | custom-call | tf_op jit(solution)/shard_map/pallas_call | solution.py:140
  406.4 4.0 convolution_convert_fusion.3
  410.4 2.8 convolution_convert_fusion.2
  413.1 2.7 convolution_convert_fusion.4
  415.9 5.1 fusion.21
  421.6 208.5 %reduce.5 = (f32[2,256,2816]{2,1,0:T(8,128)}, f32[256,2816]{1,0:T(8,128)}, f32[16,1024]{1,0:T(8,128)}, f32[32,1024]{1,0:T(8,128)}, f32[32,1024]{1,0:T(8,128)}, /*index=5*/f32[32,1024]{1,0:T(8,128)}, f32[32,1024]{1,0:T(8,128)}) custom-call(bf16[33,4,256,256]{3,2,1,0:T(8,128)(2,1)} %get-tuple-element.33.refs_0_, f32[16,1024]{1,0:T(8,128)} %pad.10.refs_1_, ...), custom_call_target="tpu_custom_call" | custom-call | tf_op jit(solution)/shard_map/reduce/pallas_call | solution.py:627
  630.1 0.7 slice_reduce_fusion
  630.8 1.4 fusion.60
  632.2 1.4 slice_bitcast_fusion
  634.4 3.5 copy.35
  637.9 3.5 fusion.20
  641.5 0.8 pad_maximum_fusion
  642.9 5.5 copy.44
  (81 shorter events, 6.4 us)
Async XLA Ops:
  7.2 137.3 %copy-start = (f32[1024,8]{0,1:T(8,128)S(1)}, f32[1024,8]{0,1:T(8,128)}, u32[]{:S(2)}) copy-start(f32[1024,8]{0,1:T(8,128)} %param.20) | copy-start | bytes 98308
  7.2 76.0 %copy-start.7 = (bf16[512,1024]{1,0:T(8,128)(2,1)S(1)}, bf16[512,1024]{1,0:T(8,128)(2,1)}, u32[]{:S(2)}) copy-start(bf16[512,1024]{1,0:T(8,128)(2,1)} %param.12) | copy-start | bytes 3145732
  7.2 4.2 copy-start.20
  7.2 4.3 copy-start.18
  7.2 76.0 %copy-start.19 = (f32[1024]{0:T(1024)S(1)}, f32[1024]{0:T(1024)}, u32[]{:S(2)}) copy-start(f32[1024]{0:T(1024)} %param.15) | copy-start | bytes 12292
  7.2 76.0 %all-gather.3.cloned.1.call-start = ((), (), s32[]{:S(2)}) async-start(), calls=%async_computation | async-start | bytes 6488064 | tf_op jit(solution)/shard_map/all_gather | solution.py:703
  8.0 133.3 %all-gather.5.cloned.1.call-start = ((), (), s32[]{:S(2)}) async-start(), calls=%async_computation.1 | async-start | bytes 2162688 | tf_op jit(solution)/shard_map/all_gather | solution.py:704
  105.2 1.7 copy-start.2
  141.2 3.0 copy-start.17
  144.2 1.3 copy-start.3
  144.2 1.3 copy-start.16
  145.6 3.1 copy-start.10
  373.2 3.5 copy-start.21
  376.6 1.6 copy-start.4
  376.7 1.8 copy-start.11
  385.2 2.7 copy-start.5
  385.2 2.7 copy-start.22
  406.4 4.0 copy-start.8
  410.4 5.5 slice-start
  413.1 2.7 slice-start.1
  634.4 3.5 copy-start.6
  634.4 3.5 copy-start.9
  637.9 3.5 copy-start.13
  637.9 3.5 copy-start.14
  637.9 3.5 copy-start.15
  637.9 4.3 copy-start.12
  642.9 5.5 copy-start.1
Sparse Core Ops, SparseCore 0:
  11.1 72.1 all-gather.2
  86.2 54.9 all-gather.4

commit v3 on v1

v3 whole, which is shorter than its diff:
```python
import functools

import jax
import jax.numpy as jnp
from jax import lax
from jax.experimental import pallas as pl
from jax.experimental.pallas import tpu as pltpu
from jax.sharding import PartitionSpec as P

LENGTH = 512
EPS = 1e-06
HIGHEST = lax.Precision.HIGHEST
F32 = jnp.float32
BF16 = jnp.bfloat16


def dot_nt(a, b):
    return lax.dot_general(a, b, (((1,), (1,)), ((), ())), preferred_element_type=F32)


def dot_nn(a, b):
    return jnp.dot(a, b, preferred_element_type=F32)


def iota(shape, axis):
    return lax.broadcasted_iota(jnp.int32, shape, axis)


def spread_bias(row):
    values = jnp.broadcast_to(row, (8, 1024))
    lift = 7 - iota((8, 1024), 0)
    for bit in (1, 2, 4):
        values = jnp.where((lift // bit) % 2 == 1, pltpu.roll(values, 1024 - bit, 1), values)
    return jnp.concatenate(
        [pltpu.roll(values, (904 + 8 * block) % 1024, 1) for block in range(16)], axis=0
    )


def fold_bias(parts):
    total = parts[0:8]
    total = pltpu.roll(total, 120, 1)
    for block in range(1, 16):
        piece = parts[8 * block : 8 * block + 8]
        total = total + (pltpu.roll(piece, 120 - 8 * block, 1) if block < 15 else piece)
    lift = 7 - iota((8, 1024), 0)
    for bit in (1, 2, 4):
        total = jnp.where((lift // bit) % 2 == 1, pltpu.roll(total, bit, 1), total)
    return jnp.sum(total, axis=0, keepdims=True)


MESH = pl.DeviceIdType.MESH
ANY = pl.BlockSpec(memory_space=pl.ANY)
GROUPS = 4
TILE = 256


def flip(index, mask):
    bit = 1
    while bit <= mask:
        if mask & bit:
            index = index + bit - 2 * bit * ((index // bit) % 2)
        bit *= 2
    return index


def remote(src, dst, send_sem, recv_sem, **axes):
    return pltpu.make_async_remote_copy(
        src_ref=src,
        dst_ref=dst,
        send_sem=send_sem,
        recv_sem=recv_sem,
        device_id=axes,
        device_id_type=MESH,
    )


def greet(partners):
    barrier = pltpu.get_barrier_semaphore()
    for axes in partners:
        pl.semaphore_signal(barrier, inc=1, device_id=axes, device_id_type=MESH)
    pl.semaphore_wait(barrier, len(partners))


def gelu_parts(x):
    root = 0.7978845608028654
    square = x * x
    t = jnp.tanh(root * x * (1.0 + 0.044715 * square))
    half = 0.5 * (1.0 + t)
    slope = half + 0.5 * x * (1.0 - t * t) * (root * (1.0 + 3 * 0.044715 * square))
    return x * half, slope


def experts_kernel(
    xs_ref,
    gates_ref,
    g_ref,
    w_in_ref,
    w_out_ref,
    y_ref,
    dx_back_ref,
    dgates_back_ref,
    dw_ref,
    w_in_v,
    w_out_v,
    x_v,
    gates_v,
    dgates_v,
    g_v,
    dy_v,
    hid_v,
    dgate_v,
    dup_v,
    y_v,
    dx_v,
    y_sum,
    dx_sum,
    stage,
    local_sem,
    stage_sem,
    x_send,
    x_recv,
    gates_send,
    gates_recv,
    dgates_send,
    dgates_recv,
    dx_send,
    dx_recv,
    y_sem,
):
    expert_count, capacity, width = xs_ref.shape
    hidden = w_out_ref.shape[0]
    tiles = hidden // TILE
    size = expert_count // GROUPS
    rows = size * capacity
    me = lax.axis_index("expert")
    my_group, my_place = me // size, me % size

    def others(c):
        group = flip(my_group, c)
        return [group * size + (my_place + s) % size for s in range(1 if c == 0 else 0, size)]

    greet([{"expert": (me + d) % expert_count} for d in range(1, expert_count)])
    for c in (2, 3, 1, 0):
        for peer in others(c):
            remote(
                xs_ref.at[peer], x_v.at[me], x_send.at[peer], x_recv.at[me], expert=peer
            ).start()
            remote(
                gates_ref.at[peer], gates_v.at[me], gates_send.at[peer], gates_recv.at[me], expert=peer
            ).start()
    own = [
        pltpu.make_async_copy(xs_ref.at[me], x_v.at[me], local_sem.at[0]),
        pltpu.make_async_copy(gates_ref.at[me], gates_v.at[me], local_sem.at[1]),
        pltpu.make_async_copy(g_ref, g_v, local_sem.at[4]),
        pltpu.make_async_copy(w_in_ref, w_in_v, local_sem.at[2]),
        pltpu.make_async_copy(w_out_ref, w_out_v, local_sem.at[3]),
    ]
    for copy in own:
        copy.start()
    for copy in own:
        copy.wait()

    def y_copy(c):
        span = pl.ds(flip(my_group, c) * size, size)
        return pltpu.make_async_copy(y_v.at[span], y_ref.at[span], y_sem.at[c])

    def back_copies(peer, at):
        return [
            remote(
                dx_v.at[peer], dx_back_ref.at[at], dx_send.at[peer], dx_recv.at[at], expert=peer
            ),
            remote(
                dgates_v.at[peer],
                dgates_back_ref.at[at],
                dgates_send.at[peer],
                dgates_recv.at[at],
                expert=peer,
            ),
        ]

    dgates_v[...] = jnp.zeros_like(dgates_v)
    for c in range(GROUPS):
        group = flip(my_group, c)
        span = pl.ds(group * size, size)
        for peer in others(c):
            remote(
                xs_ref.at[peer], x_v.at[peer], x_send.at[peer], x_recv.at[peer], expert=peer
            ).wait_recv()
            remote(
                gates_ref.at[peer], gates_v.at[peer], gates_send.at[peer], gates_recv.at[peer], expert=peer
            ).wait_recv()
        for s in range(size):
            src = group * size + s
            gate_col = gates_v[src].T[0:capacity, 0:1]
            dy_v[src] = (g_v[src].astype(F32) * gate_col).astype(BF16)
        y_sum[...] = jnp.zeros_like(y_sum)
        dx_sum[...] = jnp.zeros_like(dx_sum)

        def step(f, carry, group=group, span=span):
            cols = pl.ds(pl.multiple_of(f * TILE, TILE), TILE)
            x = x_v[span].reshape(rows, width)
            dy = dy_v[span].reshape(rows, width)
            w_gate, w_up, w_down = w_in_v[0, :, cols], w_in_v[1, :, cols], w_out_v[cols, :]
            gate, up, dhid = dot_nn(x, w_gate), dot_nn(x, w_up), dot_nt(dy, w_down)
            gelu, slope = gelu_parts(gate)
            hid = (gelu * up).astype(BF16)
            dgate = (dhid * up * slope).astype(BF16)
            dup = (dhid * gelu).astype(BF16)
            hid_v[group, :, cols] = hid
            dgate_v[group, :, cols] = dgate
            dup_v[group, :, cols] = dup
            y_sum[...] += dot_nn(hid, w_down)
            dx_sum[...] += dot_nt(dgate, w_gate) + dot_nt(dup, w_up)
            return carry

        lax.fori_loop(0, tiles, step, 0)
        y_v[span] = y_sum[...].astype(BF16).reshape(size, capacity, width)
        dx_v[span] = dx_sum[...].astype(BF16).reshape(size, capacity, width)
        y_copy(c).start()
        for s in range(size):
            src = group * size + s
            product = g_v[src].astype(F32) * y_v[src].astype(F32)
            dgate = jnp.sum(product, axis=1, keepdims=True)
            dgates_v[src, :, 0:capacity] = jnp.broadcast_to(dgate, (capacity, 128)).T[0:8]
        for peer in others(c):
            for copy in back_copies(peer, me):
                copy.start()
    own = [
        pltpu.make_async_copy(dx_v.at[me], dx_back_ref.at[me], local_sem.at[0]),
        pltpu.make_async_copy(dgates_v.at[me], dgates_back_ref.at[me], local_sem.at[1]),
    ]
    for copy in own:
        copy.start()

    slots = expert_count * capacity
    w_in_v[0, :, 0:slots] = x_v[...].reshape(slots, width).T
    w_in_v[1, :, 0:slots] = dy_v[...].reshape(slots, width).T

    def put(m, f):
        return pltpu.make_async_copy(stage.at[m], dw_ref.at[m * tiles + f], stage_sem.at[m])

    def grads(f, carry):
        cols = pl.ds(pl.multiple_of(f * TILE, TILE), TILE)
        for m, (side, right) in enumerate(((0, dgate_v), (0, dup_v), (1, hid_v))):

            @pl.when(f > 0)
            def _():
                put(m, f - 1).wait()

            block = dot_nn(w_in_v[side, :, 0:slots], right[:, :, cols].reshape(slots, TILE))
            stage[m] = block.astype(BF16).reshape(stage.shape[1:])
            put(m, f).start()
        return carry

    lax.fori_loop(0, tiles, grads, 0)
    for m in range(3):
        put(m, tiles - 1).wait()
    for copy in own:
        copy.wait()
    for c in range(GROUPS):
        for peer in others(c):
            for src, dst, send_sem, recv_sem in (
                (xs_ref, x_v, x_send, x_recv),
                (gates_ref, gates_v, gates_send, gates_recv),
            ):
                remote(
                    src.at[peer], dst.at[me], send_sem.at[peer], recv_sem.at[me], expert=peer
                ).wait_send()
            for copy in back_copies(peer, me):
                copy.wait_send()
            for copy in back_copies(peer, peer):
                copy.wait_recv()
        y_copy(c).wait()


def experts(xs, gates, g, w_in, w_out, dp_count):
    expert_count, capacity, width = xs.shape
    hidden = w_out.shape[0]
    size = expert_count // GROUPS
    tiles = hidden // TILE
    rows = size * capacity
    slots = jax.ShapeDtypeStruct(xs.shape, BF16)
    parts = (dp_count, width // dp_count, TILE)
    peers = pltpu.SemaphoreType.DMA((expert_count,))
    return pl.pallas_call(
        experts_kernel,
        in_specs=[ANY] * 5,
        out_specs=[ANY] * 4,
        out_shape=[slots, slots, jax.ShapeDtypeStruct(gates.shape, F32), jax.ShapeDtypeStruct((3 * tiles, *parts), BF16)],
        scratch_shapes=[
            pltpu.VMEM(w_in.shape, BF16),
            pltpu.VMEM(w_out.shape, BF16),
            pltpu.VMEM(xs.shape, BF16),
            pltpu.VMEM(gates.shape, F32),
            pltpu.VMEM(gates.shape, F32),
            pltpu.VMEM(xs.shape, BF16),
            pltpu.VMEM(xs.shape, BF16),
            pltpu.VMEM((GROUPS, rows, hidden), BF16),
            pltpu.VMEM((GROUPS, rows, hidden), BF16),
            pltpu.VMEM((GROUPS, rows, hidden), BF16),
            pltpu.VMEM(xs.shape, BF16),
            pltpu.VMEM(xs.shape, BF16),
            pltpu.VMEM((rows, width), F32),
            pltpu.VMEM((rows, width), F32),
            pltpu.VMEM((3, *parts), BF16),
            pltpu.SemaphoreType.DMA((5,)),
            pltpu.SemaphoreType.DMA((3,)),
        ]
        + [peers] * 8
        + [pltpu.SemaphoreType.DMA((GROUPS,))],
        compiler_params=pltpu.CompilerParams(
            collective_id=1, has_side_effects=True, vmem_limit_bytes=61 * 1024 * 1024
        ),
        name="experts",
    )(xs, gates, g, w_in, w_out)


def column(values, k):
    return values[:, k : k + 1]


def attend_pair(j, a, qkv_v, table_ref, p_ref):
    def lanes(part):
        return pl.ds(pl.multiple_of(256 * part + 128 * a, 128), 128)

    query = qkv_v[j, :, lanes(0)] * jnp.asarray(0.125, BF16)
    values_t = qkv_v[j, :, lanes(2)].T
    half = iota((512, 128), 1) // 64
    halves = []
    for t in range(2):
        shifted = spread_bias(table_ref[pl.ds(4 * j + 2 * a + t, 1), :])
        query_t = jnp.where(half == t, query, jnp.zeros_like(query))
        scores = [
            dot_nt(qkv_v[j, 128 * c : 128 * c + 128, lanes(1)], query_t)
            + shifted[:, 384 - 128 * c : 896 - 128 * c]
            for c in range(4)
        ]
        top = functools.reduce(jnp.maximum, [jnp.max(s, axis=0, keepdims=True) for s in scores])
        exps = [jnp.exp(s - top) for s in scores]
        total = functools.reduce(jnp.add, [jnp.sum(e, axis=0, keepdims=True) for e in exps])
        inverse = 1.0 / total
        for c in range(4):
            p_ref[t, 128 * c : 128 * c + 128, :] = (exps[c] * inverse).astype(BF16)
        halves.append(dot_nn(values_t, p_ref[t]))
    return jnp.where(iota((128, 512), 0) < 64, halves[0], halves[1])


def front_kernel(
    tokens_ref,
    gain1_ref,
    gain2_ref,
    table_ref,
    routes_ref,
    grad_ref,
    router_ref,
    ws_ref,
    wo_ref,
    wq_out,
    wo_out,
    qkv_out,
    p_out,
    g_back,
    mixed_t_ref,
    normed_t_ref,
    resid_ref,
    normed2_ref,
    xs_ref,
    gates_ref,
    cols_ref,
    wq_v,
    wo_v,
    qkv_v,
    p_v,
    mixed_v,
    normed_v,
    hot_v,
    g_v,
    own_sem,
    z_send,
    z_recv,
    xy_send,
    xy_recv,
    core_send,
    core_recv,
    g_send,
    g_recv,
    out_sem,
    p_sem,
):
    expert_count, capacity, width = xs_ref.shape
    lane_count = gates_ref.shape[2]
    slots = expert_count * capacity
    size = expert_count // GROUPS
    chips = expert_count // 2
    me, dp = lax.axis_index("expert"), lax.axis_index("dp")
    core, chip = me % 2, me // 2
    x, y = dp % 2, dp // 2
    core_peer = me + 1 - 2 * core
    x_peer, y_peer = dp + 1 - 2 * x, dp + 2 - 4 * y
    my_group, my_place = me // size, me % size
    chip_peers = [(chip + d) % chips for d in range(1, chips)]
    greet(
        [{"expert": (me + d) % expert_count} for d in range(1, expert_count)]
        + [{"dp": x_peer}, {"dp": y_peer}]
    )

    groups = ws_ref.shape[0]
    count = groups + 1
    srcs = [ws_ref.at[j] for j in range(groups)] + [wo_ref]
    bufs = [wq_v.at[j] for j in range(groups)] + [wo_v]
    widths = [ws_ref.shape[2]] * groups + [wo_ref.shape[1]]
    places = ((y, x), (y, 1 - x), (1 - y, x), (1 - y, 1 - x))

    def z_copy(j, peer, at):
        return remote(
            srcs[j], bufs[j].at[y, x, at, core], z_send.at[j, peer], z_recv.at[j, at], expert=peer * 2 + core
        )

    def own_copy(j):
        return pltpu.make_async_copy(srcs[j], bufs[j].at[y, x, chip, core], own_sem.at[j])

    def xy_copy(j, k):
        half = widths[j] // 2
        src = (
            bufs[j].at[y, x, :, core],
            bufs[j].at[y, x, :, core],
            bufs[j].at[1 - y, x, :, core, :, half : 2 * half],
            bufs[j].at[y, 1 - x, :, core, :, 0:half],
        )[k]
        return remote(src, src, xy_send.at[j, k], xy_recv.at[j, k], dp=(x_peer, y_peer)[k % 2])

    def core_copy(j, k):
        src = bufs[j].at[places[k][0], places[k][1], :, core]
        return remote(src, src, core_send.at[j, k], core_recv.at[j, k], expert=core_peer)

    def spread(j):
        own_copy(j).wait()
        for peer in chip_peers:
            z_copy(j, peer, peer).wait_recv()
        for k in range(2):
            xy_copy(j, k).start()
        core_copy(j, 0).start()

    def forward(j):
        for k in range(2):
            xy_copy(j, k).wait_recv()
            xy_copy(j, 3 - k).start()
            core_copy(j, 1 + k).start()

    def complete(j):
        for k in (2, 3):
            xy_copy(j, k).wait_recv()
        core_copy(j, 3).start()

    def out_copy(j):
        src, dst = (wq_v.at[j], wq_out.at[j]) if j < groups else (wo_v, wo_out)
        return pltpu.make_async_copy(src, dst, out_sem.at[j])

    def gathered(j):
        for k in range(4):
            core_copy(j, k).wait_recv()
        out_copy(j).start()

    for j in range(count):
        own_copy(j).start()
        for peer in chip_peers:
            z_copy(j, peer, chip).start()

    inputs = tokens_ref[...].astype(F32)
    inv_rms = lax.rsqrt(jnp.mean(inputs * inputs, axis=1, keepdims=True) + EPS)
    normed = (inputs * inv_rms * gain1_ref[...]).astype(BF16)
    normed_v[...] = normed
    normed_t_ref[...] = normed.T
    spread(0)
    spread(1)

    routes = routes_ref[...]
    rows = routes.shape[0]
    lane = iota((rows, 128), 1)
    hots = [lane == column(routes, k) for k in range(2)]
    earlier = (iota((rows, rows), 0) > iota((rows, rows), 1)).astype(BF16)
    ones = [jnp.where(h, 1.0, 0.0) for h in hots]
    counts = [dot_nn(earlier, o.astype(BF16)) for o in ones]
    counts[1] = counts[1] + jnp.sum(ones[0], axis=0, keepdims=True)
    slot = []
    for k in range(2):
        place = jnp.sum(counts[k] * ones[k], axis=1, keepdims=True)
        at = column(routes, k).astype(F32) * capacity + place
        slot.append(jnp.where(place < capacity, at, float(slots)))
    slot_rows = jnp.where(lane == 0, slot[0], slot[1]).T
    slot_ids = iota((slots, rows), 0).astype(F32)
    hot = (slot_ids == slot_rows[0:1]) | (slot_ids == slot_rows[1:2])
    hot_v[...] = jnp.where(hot, 1.0, 0.0).astype(BF16)
    g_v[...] = dot_nn(hot_v[...], grad_ref[...]).astype(BF16).reshape(g_v.shape)

    def g_copy(peer, at):
        return remote(g_v.at[peer], g_back.at[at], g_send.at[peer], g_recv.at[at], expert=peer)

    def others(c):
        group = flip(my_group, c)
        return [group * size + (my_place + s) % size for s in range(1 if c == 0 else 0, size)]

    peers = [peer for c in (2, 3, 1, 0) for peer in others(c)]
    for peer in peers:
        g_copy(peer, me).start()
    g_own = pltpu.make_async_copy(g_v.at[me], g_back.at[me], own_sem.at[count])
    g_own.start()

    def p_copy(j, a):
        return pltpu.make_async_copy(p_v.at[a], p_out.at[pl.ds(4 * j + 2 * a, 2)], p_sem.at[a])

    def group(j):
        gathered(j)
        qkv_v[j] = dot_nn(normed_v[...], wq_v[j].reshape(width, widths[j])).astype(BF16)

        def pair(a, carry):
            if j > 0:
                p_copy(j - 1, a).wait()
            mixed = attend_pair(j, a, qkv_v, table_ref, p_v.at[a])
            p_copy(j, a).start()
            span = pl.ds(pl.multiple_of(256 * j + 128 * a, 128), 128)
            mixed_t_ref[span, :] = mixed.astype(BF16)
            mixed_v[:, span] = mixed.T.astype(BF16)
            return carry

        lax.fori_loop(0, 2, pair, 0)

    forward(0)
    spread(2)
    spread(3)
    forward(1)
    complete(0)
    spread(4)
    forward(2)
    complete(1)
    group(0)
    forward(3)
    complete(2)
    group(1)
    forward(4)
    complete(3)
    group(2)
    complete(4)
    group(3)
    qkv_copy = pltpu.make_async_copy(qkv_v, qkv_out, own_sem.at[count + 1])
    qkv_copy.start()
    gathered(groups)

    resid = tokens_ref[...].astype(F32) + dot_nn(mixed_v[...], wo_v[...].reshape(width, width))
    resid_ref[...] = resid
    inv_rms2 = lax.rsqrt(jnp.mean(resid * resid, axis=1, keepdims=True) + EPS)
    normed2 = (resid * inv_rms2 * gain2_ref[...]).astype(BF16)
    normed2_ref[...] = normed2
    xs_ref[...] = dot_nn(hot_v[...], normed2).astype(BF16).reshape(xs_ref.shape)
    rest = router_ref[...]
    logits = jnp.zeros((rows, expert_count), F32)
    for _ in range(3):
        piece = rest.astype(BF16)
        rest = rest - piece.astype(F32)
        logits = logits + dot_nn(normed2, piece)
    ids = iota((rows, expert_count), 1)
    chosen = [
        jnp.sum(jnp.where(ids == column(routes, k), logits, 0.0), axis=1, keepdims=True)
        for k in range(2)
    ]
    top = jnp.maximum(chosen[0], chosen[1])
    exps = [jnp.exp(c - top) for c in chosen]
    gates = [e / (exps[0] + exps[1]) for e in exps]
    cols = jnp.where(lane == 2, gates[0], jnp.where(lane == 3, gates[1], 0.0))
    cols_ref[...] = jnp.where(lane == 0, slot[0], jnp.where(lane == 1, slot[1], cols))
    wide = iota((rows, lane_count), 1)

    def gate_row(e, carry):
        base = (e * capacity).astype(F32)
        total = jnp.zeros((rows, lane_count), F32)
        for k in range(2):
            here = (wide.astype(F32) == slot[k] - base) & (wide < capacity)
            total = total + jnp.where(here, gates[k], 0.0)
        row = jnp.sum(total, axis=0, keepdims=True)
        gates_ref[pl.ds(e, 1)] = jnp.broadcast_to(row, (8, lane_count))[None]
        return carry

    lax.fori_loop(0, expert_count, gate_row, 0)

    for a in range(2):
        p_copy(groups - 1, a).wait()
    qkv_copy.wait()
    g_own.wait()
    for j in range(count):
        out_copy(j).wait()
        for peer in chip_peers:
            z_copy(j, peer, chip).wait_send()
        for k in range(4):
            xy_copy(j, k).wait_send()
            core_copy(j, k).wait_send()
    for peer in peers:
        g_copy(peer, me).wait_send()
        g_copy(peer, peer).wait_recv()


def front(tokens, gain1, gain2, table, routes, grad_out, router, ws, wo, dp_count, capacity):
    rows, width = tokens.shape
    expert_count = router.shape[1]
    chips = expert_count // 2
    groups, own, part = ws.shape
    heads = table.shape[0]
    lane_count = -(-capacity // 128) * 128
    vmem = pl.BlockSpec(memory_space=pltpu.VMEM)
    sem = pltpu.SemaphoreType.DMA
    shape = jax.ShapeDtypeStruct
    slots = (expert_count, capacity, width)
    spread = (2, 2, chips, 2, own)
    return pl.pallas_call(
        front_kernel,
        in_specs=[vmem] * 9,
        out_specs=[ANY] * 5 + [vmem] * 7,
        out_shape=[
            shape((groups, *spread, part), BF16),
            shape((*spread, width), BF16),
            shape((groups, rows, part), BF16),
            shape((heads, rows, rows), BF16),
            shape(slots, BF16),
            shape((width, rows), BF16),
            shape((width, rows), BF16),
            shape((rows, width), F32),
            shape((rows, width), BF16),
            shape(slots, BF16),
            shape((expert_count, 8, lane_count), F32),
            shape((rows, 128), F32),
        ],
        scratch_shapes=[
            pltpu.VMEM((groups, *spread, part), BF16),
            pltpu.VMEM((*spread, width), BF16),
            pltpu.VMEM((groups, rows, part), BF16),
            pltpu.VMEM((2, 2, rows, rows), BF16),
            pltpu.VMEM((rows, width), BF16),
            pltpu.VMEM((rows, width), BF16),
            pltpu.VMEM((expert_count * capacity, rows), BF16),
            pltpu.VMEM(slots, BF16),
            sem((groups + 3,)),
            sem((groups + 1, chips)),
            sem((groups + 1, chips)),
            sem((groups + 1, 4)),
            sem((groups + 1, 4)),
            sem((groups + 1, 4)),
            sem((groups + 1, 4)),
            sem((expert_count,)),
            sem((expert_count,)),
            sem((groups + 1,)),
            sem((2,)),
        ],
        compiler_params=pltpu.CompilerParams(
            collective_id=3, has_side_effects=True, vmem_limit_bytes=60 * 1024 * 1024
        ),
        name="front",
    )(tokens, gain1, gain2, table, routes, grad_out, router, ws, wo)


def attend_back_pair(j, a, qkv_v, p_ref, grads_v, dqkv_v, fold_ref):
    def lanes(part):
        return pl.ds(pl.multiple_of(256 * part + 128 * a, 128), 128)

    query = qkv_v[j, :, lanes(0)] * jnp.asarray(0.125, BF16)
    keys_t = qkv_v[j, :, lanes(1)].T
    values = qkv_v[j, :, lanes(2)]
    grads = grads_v[:, pl.ds(pl.multiple_of(256 * j + 128 * a, 128), 128)]
    half = iota((512, 128), 1) // 64
    dq_halves, dk_halves, dv_halves = [], [], []
    for t in range(2):
        values_t = jnp.where(half == t, values, jnp.zeros_like(values))
        probs = [p_ref[t, 128 * c : 128 * c + 128, :].astype(F32) for c in range(4)]
        grad_probs = [dot_nt(values_t[128 * c : 128 * c + 128], grads) for c in range(4)]
        delta = functools.reduce(
            jnp.add,
            [jnp.sum(p * g, axis=0, keepdims=True) for p, g in zip(probs, grad_probs)],
        )
        scores = [(p * (g - delta)).astype(BF16) for p, g in zip(probs, grad_probs)]
        padded = [
            jnp.concatenate(
                ([jnp.zeros((128, 384 - 128 * c), F32)] if c < 3 else [])
                + [scores[c].astype(F32), jnp.zeros((128, 128 + 128 * c), F32)],
                axis=1,
            )
            for c in range(4)
        ]
        fold_ref[pl.ds(4 * j + 2 * a + t, 1), :] = fold_bias(functools.reduce(jnp.add, padded))
        grad_scores = jnp.concatenate(scores, axis=0)
        dv_halves.append(dot_nn(p_ref[t], grads))
        dk_halves.append(dot_nn(grad_scores, query))
        dq_halves.append(dot_nn(keys_t, grad_scores))
    dq = jnp.where(iota((128, 512), 0) < 64, dq_halves[0], dq_halves[1]) * 0.125
    dqkv_v[:, lanes(0)] = dq.T.astype(BF16)
    dqkv_v[:, lanes(1)] = jnp.where(half == 0, dk_halves[0], dk_halves[1]).astype(BF16)
    dqkv_v[:, lanes(2)] = jnp.where(half == 0, dv_halves[0], dv_halves[1]).astype(BF16)


def dot_exact(a, b, dot=dot_nn):
    total = None
    for _ in range(3):
        piece = a.astype(BF16)
        a = a - piece.astype(F32)
        term = dot(piece, b)
        total = term if total is None else total + term
    return total


def dot_f32(a, b):
    total = None
    for _ in range(3):
        piece = b.astype(BF16)
        b = b - piece.astype(F32)
        term = dot_exact(a, piece)
        total = term if total is None else total + term
    return total


BATCH = 3


def back_kernel(
    dw_ref,
    ys_ref,
    dx_ref,
    dgates_ref,
    cols_ref,
    routes_ref,
    tokens_ref,
    grad_ref,
    resid_ref,
    normed2_ref,
    normed_t_ref,
    mixed_t_ref,
    gain1_ref,
    gain2_ref,
    router_t_ref,
    bucket_hot_ref,
    wq_ref,
    wo_ref,
    qkv_ref,
    p_ref,
    w_out_ref,
    first_ref,
    second_ref,
    small_out_ref,
    gq_out_ref,
    go_out_ref,
    block_ref,
    grad_tokens_ref,
    y_v,
    grads_q,
    grads_o,
    core_q,
    core_o,
    step1_q,
    step1_o,
    step2_q,
    step2_o,
    last_q,
    last_o,
    qkv_v,
    p_v,
    wq_v,
    dqkv_v,
    dmix_v,
    dn1_v,
    fold_v,
    small_v,
    own_v,
    first_v,
    second_v,
    pass_v,
    total_v,
    y_send,
    y_recv,
    first_send,
    first_recv,
    second_send,
    second_recv,
    ring_sem,
    total_sem,
    small_send,
    small_recv,
    core_send,
    core_recv,
    step1_send,
    step1_recv,
    step2_send,
    step2_recv,
    last_send,
    last_recv,
    local_sem,
    p_sem,
    wq_sem,
):
    expert_count, capacity, width = ys_ref.shape
    slots = expert_count * capacity
    rows = tokens_ref.shape[0]
    chips = expert_count // 2
    size = expert_count // GROUPS
    me, dp = lax.axis_index("expert"), lax.axis_index("dp")
    core, chip = me % 2, me // 2
    x, y = dp % 2, dp // 2
    core_peer = me + 1 - 2 * core
    x_peer, y_peer = dp + 1 - 2 * x, dp + 2 - 4 * y
    my_group, my_place = me // size, me % size
    chip_peers = [(chip + d) % chips for d in range(1, chips)]
    greet(
        [{"expert": (me + d) % expert_count} for d in range(1, expert_count)]
        + [{"dp": x_peer}, {"dp": y_peer}]
    )

    tile_count = dw_ref.shape[0]
    tiles = tile_count // 3
    batches = tile_count // BATCH

    def way(t):
        q = t % 2
        sent = [(1 - q) * (2 * i + 1 - x) + q * (2 * (1 - y) + i) for i in range(2)]
        peer1 = (1 - q) * x_peer + q * y_peer
        peer2 = (1 - q) * y_peer + q * x_peer
        keep = (1 - q) * y + q * x
        held = [(1 - q) * (2 * k + x) + q * (2 * y + k) for k in (keep, 1 - keep)]
        return sent, held, peer1, peer2, keep

    def first_copy(t, i):
        sent, _, peer, _, _ = way(t)
        return remote(
            dw_ref.at[t, sent[i]], first_ref.at[t, i], first_send.at[t, i], first_recv.at[t, i], dp=peer
        )

    def second_copy(t, n):
        peer = way(t)[3]
        return remote(
            pass_v.at[n % 2, t % BATCH], second_ref.at[t], second_send.at[t], second_recv.at[t], dp=peer
        )

    def ring(src, dst, slot, q, k):
        return pltpu.make_async_copy(src, dst.at[slot, q], ring_sem.at[slot, q, k])

    def relay_loads(t, b):
        _, held, _, _, keep = way(t)
        q = t % BATCH
        return [
            ring(dw_ref.at[t, held[1]], own_v, b % 2, q, 0),
            ring(first_ref.at[t, 1 - keep], first_v, b % 2, q, 1),
        ]

    def finish_loads(t, b):
        _, held, _, _, keep = way(t)
        q = t % BATCH
        return [
            ring(dw_ref.at[t, held[0]], own_v, b % 2, q, 0),
            ring(first_ref.at[t, keep], first_v, b % 2, q, 1),
            ring(second_ref.at[t], second_v, b % 2, q, 2),
        ]

    def over(b, body):
        def step(t, carry):
            body(t)
            return carry

        lax.fori_loop(BATCH * b, BATCH * b + BATCH, step, 0)

    def issue(b):
        def body(t):
            for i in range(2):
                first_copy(t, i).start()

        over(b, body)

    def relay_begin(b):
        def body(t):
            for i in range(2):
                first_copy(t, i).wait_recv()
            for load in relay_loads(t, b):
                load.start()

        over(b, body)

    def relay_end(b):
        def body(t):
            for load in relay_loads(t, b):
                load.wait()
            if b >= 2:
                second_copy(t - 2 * BATCH, b).wait_send()
            q = t % BATCH
            pass_v[b % 2, q] = (
                own_v[b % 2, q].astype(F32) + first_v[b % 2, q].astype(F32)
            ).astype(BF16)
            second_copy(t, b).start()

        over(b, body)

    def finish_begin(b):
        def body(t):
            second_copy(t, b).wait_recv()
            for load in finish_loads(t, b):
                load.start()

        over(b, body)

    def total_copy(t, b):
        span = pl.ds(pl.multiple_of((t % tiles) * TILE, TILE), TILE)
        q = t % BATCH
        return pltpu.make_async_copy(
            total_v.at[b % 2, q], w_out_ref.at[t // tiles, :, span], total_sem.at[b % 2, q]
        )

    def finish_end(b):
        def body(t):
            for load in finish_loads(t, b):
                load.wait()
            if b >= 2:
                total_copy(t - 2 * BATCH, b).wait()
            q = t % BATCH
            total = own_v[b % 2, q].astype(F32) + first_v[b % 2, q].astype(F32)
            total_v[b % 2, q] = total + second_v[b % 2, q].astype(F32)
            total_copy(t, b).start()

        over(b, body)

    groups = grads_q.shape[0]
    count = groups + 1

    def pick(many, one, p):
        return many.at[p] if p < groups else one

    grads = [pick(grads_q, grads_o, p) for p in range(count)]
    cores = [pick(core_q, core_o, p) for p in range(count)]
    step1 = [pick(step1_q, step1_o, p) for p in range(count)]
    step2 = [pick(step2_q, step2_o, p) for p in range(count)]
    lasts = [pick(last_q, last_o, p) for p in range(count)]
    outs = [pick(gq_out_ref, go_out_ref, p) for p in range(count)]
    widths = [grads_q.shape[-1]] * groups + [grads_o.shape[-1]]

    def part_core(p):
        return remote(
            grads[p].at[:, :, :, 1 - core], cores[p], core_send.at[p], core_recv.at[p], expert=core_peer
        )

    def part_step1(p, b):
        half = widths[p] // 2
        src = (
            grads[p].at[:, 1 - x, :, core, :, 0:half]
            if b == 0
            else grads[p].at[1 - y, :, :, core, :, half : 2 * half]
        )
        return remote(
            src, step1[p].at[b], step1_send.at[p, b], step1_recv.at[p, b], dp=(x_peer, y_peer)[b]
        )

    def part_step2(p, b):
        src = step1[p].at[b, (1 - y, 1 - x)[b]]
        return remote(
            src, step2[p].at[b], step2_send.at[p, b], step2_recv.at[p, b], dp=(y_peer, x_peer)[b]
        )

    def part_last(p, peer, at):
        return remote(
            cores[p].at[0, 0, peer], lasts[p].at[at], last_send.at[p, peer], last_recv.at[p, at],
            expert=peer * 2 + core,
        )

    def part_a(p):
        part_core(p).start()

    def part_b(p):
        part_core(p).wait()
        total = grads[p][:, :, :, core].astype(F32) + cores[p][...].astype(F32)
        grads[p][:, :, :, core] = total.astype(BF16)
        for b in range(2):
            part_step1(p, b).start()

    def part_c(p):
        half = widths[p] // 2
        for b in range(2):
            part_step1(p, b).wait()
            for i in range(2):
                held = (
                    grads[p][i, x, :, core, :, 0:half]
                    if b == 0
                    else grads[p][y, i, :, core, :, half : 2 * half]
                )
                total = held.astype(F32) + step1[p][b, i].astype(F32)
                step1[p][b, i] = total.astype(BF16)
            part_step2(p, b).start()

    def part_d(p):
        half = widths[p] // 2
        for b in range(2):
            part_step2(p, b).wait()
            total = step1[p][b, (y, x)[b]].astype(F32) + step2[p][b].astype(F32)
            cores[p][0, 0, :, :, b * half : b * half + half] = total.astype(BF16)
        for peer in chip_peers:
            part_last(p, peer, chip).start()

    def part_e(p):
        total = cores[p][0, 0, chip].astype(F32)
        for peer in chip_peers:
            part_last(p, peer, peer).wait_recv()
            total = total + lasts[p][peer].astype(F32)
        outs[p][...] = total
        for peer in chip_peers:
            part_last(p, peer, chip).wait_send()

    partners = []
    bit = 1
    while bit < expert_count:
        partners.append({"expert": flip(me, bit)})
        bit *= 2
    partners += [{"dp": x_peer}, {"dp": y_peer}]
    stages = len(partners)

    def small_copy(s):
        return remote(
            small_v.at[0], small_v.at[1 + s], small_send.at[s], small_recv.at[s], **partners[s]
        )

    def small_next(s):
        small_copy(s).wait()
        small_v[0] = small_v[0] + small_v[1 + s]
        if s + 1 < stages:
            small_copy(s + 1).start()

    def y_copy(peer, at):
        return remote(ys_ref.at[peer], y_v.at[at], y_send.at[peer], y_recv.at[at], expert=peer)

    def others(c):
        group = flip(my_group, c)
        return [group * size + (my_place + s) % size for s in range(1 if c == 0 else 0, size)]

    peers = [peer for c in (2, 3, 1, 0) for peer in others(c)]

    def p_copy(j, a):
        return pltpu.make_async_copy(p_ref.at[pl.ds(4 * j + 2 * a, 2)], p_v.at[a], p_sem.at[a])

    def wq_copy(j):
        return pltpu.make_async_copy(wq_ref.at[j], wq_v.at[j % 2], wq_sem.at[j % 2])

    lane = iota((rows, 128), 1)
    slot = [column(cols_ref[...], k) for k in range(2)]
    gates = [column(cols_ref[...], 2 + k) for k in range(2)]

    def hots():
        at = iota((rows, slots), 1).astype(F32)
        return [at == s for s in slot]

    def dense():
        lanes = dgates_ref.shape[2]
        wide = iota((rows, lanes), 1)

        def step(e, totals):
            base = (e * capacity).astype(F32)
            row = dgates_ref[pl.ds(e, 1)][0][0:1]
            return tuple(
                totals[k]
                + jnp.where((wide.astype(F32) == slot[k] - base) & (wide < capacity), row, 0.0)
                for k in range(2)
            )

        zero = jnp.zeros((rows, lanes), F32)
        sums = lax.fori_loop(0, expert_count, step, (zero, zero))
        dgates = [jnp.sum(s, axis=1, keepdims=True) for s in sums]
        mean = gates[0] * dgates[0] + gates[1] * dgates[1]
        dchosen = [gates[k] * (dgates[k] - mean) for k in range(2)]
        routes = routes_ref[...]
        dlogits = jnp.zeros((rows, 128), F32)
        for k in range(2):
            dlogits = dlogits + jnp.where(lane == column(routes, k), dchosen[k], 0.0)
        small_rows = dot_exact(dlogits.T[0:expert_count], normed2_ref[...])
        small_v[0, 0:expert_count] = small_rows
        hot0, hot1 = hots()
        hot = jnp.where(hot0 | hot1, 1.0, 0.0).astype(BF16)
        dnormed = dot_f32(dlogits, router_t_ref[...])
        dnormed = dnormed + dot_nn(hot, dx_ref[...].reshape(slots, width))
        resid = resid_ref[...]
        inv_rms = lax.rsqrt(jnp.mean(resid * resid, axis=1, keepdims=True) + EPS)
        normed = resid * inv_rms
        scaled = dnormed * gain2_ref[...]
        small_v[0, expert_count + 1 : expert_count + 2] = jnp.sum(
            dnormed * normed, axis=0, keepdims=True
        )
        inner = jnp.mean(scaled * normed, axis=1, keepdims=True)
        dresid = grad_ref[...].astype(F32) + inv_rms * (scaled - normed * inner)
        grad_tokens_ref[...] = dresid
        dresid_r = dresid.astype(BF16)
        grads_o[...] = dot_nn(mixed_t_ref[...], dresid_r).astype(BF16).reshape(grads_o.shape)
        part_a(groups)
        dmix_v[...] = dot_nt(dresid_r, wo_ref[...]).astype(BF16)

    def group(j):
        if j + 1 < groups:
            wq_copy(j + 1).start()

        def pair(a, carry):
            p_copy(j, a).wait()
            attend_back_pair(j, a, qkv_v, p_v.at[a], dmix_v, dqkv_v, fold_v)
            if j + 1 < groups:
                p_copy(j + 1, a).start()
            return carry

        lax.fori_loop(0, 2, pair, 0)
        block = dot_nn(normed_t_ref[...], dqkv_v[...])
        grads_q[j] = block.astype(BF16).reshape(grads_q.shape[1:])
        part_a(j)
        wq_copy(j).wait()
        term = dot_nt(dqkv_v[...], wq_v[j % 2])
        dn1_v[...] = term if j == 0 else dn1_v[...] + term

    def norm_back():
        inputs = tokens_ref[...].astype(F32)
        inv_rms = lax.rsqrt(jnp.mean(inputs * inputs, axis=1, keepdims=True) + EPS)
        normed = inputs * inv_rms
        dnormed = dn1_v[...]
        scaled = dnormed * gain1_ref[...]
        small_v[0, expert_count : expert_count + 1] = jnp.sum(
            dnormed * normed, axis=0, keepdims=True
        )
        inner = jnp.mean(scaled * normed, axis=1, keepdims=True)
        grad_tokens_ref[...] += inv_rms * (scaled - normed * inner)
        buckets = dot_exact(fold_v[...], bucket_hot_ref[...], dot_nt)
        base = expert_count + 2
        heads = fold_v.shape[0]
        small_v[0, base : base + heads, 0 : buckets.shape[1]] = buckets
        small_copy(0).start()

    def outputs():
        for peer in peers:
            y_copy(peer, peer).wait_recv()
        y_own.wait()
        values = y_v[...].reshape(slots, width)
        total = resid_ref[...]
        for k, hot in enumerate(hots()):
            total = total + gates[k] * dot_nn(jnp.where(hot, 1.0, 0.0).astype(BF16), values)
        block_ref[...] = total.astype(BF16)

    small_v[0] = jnp.zeros(small_v.shape[1:], F32)
    for peer in peers:
        y_copy(peer, me).start()
    y_own = pltpu.make_async_copy(ys_ref.at[me], y_v.at[me], local_sem.at[0])
    y_own.start()
    qkv_copy = pltpu.make_async_copy(qkv_ref, qkv_v, local_sem.at[1])
    qkv_copy.start()
    wq_copy(0).start()
    for a in range(2):
        p_copy(0, a).start()
    ahead = 5
    for b in range(ahead):
        issue(b)
    dense()
    qkv_copy.wait()
    relay_begin(0)
    group(0)
    relay_end(0)
    issue(ahead)
    relay_begin(1)
    group(1)
    part_b(groups)
    relay_end(1)
    issue(ahead + 1)
    relay_begin(2)
    group(2)
    part_b(0)
    relay_end(2)
    issue(ahead + 2)
    relay_begin(3)
    group(3)
    part_b(1)
    relay_end(3)
    issue(ahead + 3)
    norm_back()
    part_b(2)
    relay_begin(4)
    relay_end(4)
    issue(ahead + 4)
    small_next(0)
    part_b(3)
    small_next(1)
    outputs()
    part_c(groups)
    relay_begin(5)
    relay_end(5)
    issue(ahead + 5)
    small_next(2)
    part_c(0)
    small_next(3)
    relay_begin(6)
    relay_end(6)
    part_c(1)
    part_d(groups)
    for s in range(4, stages):
        small_next(s)
    small_out_ref[...] = small_v[0]
    relay_begin(7)
    relay_end(7)
    part_c(2)
    part_d(0)
    part_c(3)
    part_d(1)
    relay_begin(8)
    relay_end(8)
    part_d(2)
    part_e(groups)
    relay_begin(9)
    relay_end(9)
    part_d(3)
    part_e(0)
    relay_begin(10)
    relay_end(10)
    part_e(1)
    part_e(2)
    part_e(3)
    for b in range(2):
        over(batches - 2 + b, lambda t, b=b: second_copy(t, batches - 2 + b).wait_send())
    for b in range(batches):
        finish_begin(b)
        if b > 0:
            finish_end(b - 1)
    finish_end(batches - 1)
    for b in (batches - 2, batches - 1):
        over(b, lambda t, b=b: total_copy(t, b).wait())

    def drain(t, carry):
        for i in range(2):
            first_copy(t, i).wait_send()
        return carry

    lax.fori_loop(0, tile_count, drain, 0)
    for peer in peers:
        y_copy(peer, me).wait_send()


def back(
    dw, ys, dx, dgates, cols, routes, tokens, grad_out, resid, normed2, normed_t, mixed_t,
    gain1, gain2, router_t, bucket_hot, wq, wo, qkv, probs,
):
    tile_count, dp_count, deep, _ = dw.shape
    expert_count, capacity, width = ys.shape
    chips = expert_count // 2
    rows = tokens.shape[0]
    groups, _, part = qkv.shape
    own = width // (dp_count * expert_count)
    heads = probs.shape[0]
    small_rows = -(-(expert_count + 2 + heads) // 8) * 8
    stages = expert_count.bit_length() + 1
    vmem = pl.BlockSpec(memory_space=pltpu.VMEM)
    sem = pltpu.SemaphoreType.DMA
    shape = jax.ShapeDtypeStruct
    ring = (2, BATCH, deep, TILE)

    def pairs(make):
        return [pltpu.VMEM((groups, *make(part)), BF16), pltpu.VMEM(make(width), BF16)]

    return pl.pallas_call(
        back_kernel,
        in_specs=[ANY] * 2 + [vmem] * 14 + [ANY, vmem, ANY, ANY],
        out_specs=[ANY] * 3 + [vmem] * 5,
        out_shape=[
            shape((3, deep, tile_count // 3 * TILE), F32),
            shape((tile_count, 2, deep, TILE), BF16),
            shape((tile_count, deep, TILE), BF16),
            shape((small_rows, width), F32),
            shape((groups, own, part), F32),
            shape((own, width), F32),
            shape((rows, width), BF16),
            shape((rows, width), F32),
        ],
        scratch_shapes=[pltpu.VMEM(ys.shape, BF16)]
        + pairs(lambda w: (2, 2, chips, 2, own, w))
        + pairs(lambda w: (2, 2, chips, own, w))
        + pairs(lambda w: (2, 2, chips, own, w // 2))
        + pairs(lambda w: (2, chips, own, w // 2))
        + pairs(lambda w: (chips, own, w))
        + [
            pltpu.VMEM(qkv.shape, BF16),
            pltpu.VMEM((2, 2, rows, rows), BF16),
            pltpu.VMEM((2, *wq.shape[1:]), BF16),
            pltpu.VMEM((rows, part), BF16),
            pltpu.VMEM((rows, width), BF16),
            pltpu.VMEM((rows, width), F32),
            pltpu.VMEM((heads, bucket_hot.shape[1]), F32),
            pltpu.VMEM((stages + 1, small_rows, width), F32),
            pltpu.VMEM(ring, BF16),
            pltpu.VMEM(ring, BF16),
            pltpu.VMEM(ring, BF16),
            pltpu.VMEM(ring, BF16),
            pltpu.VMEM(ring, F32),
            sem((expert_count,)),
            sem((expert_count,)),
            sem((tile_count, 2)),
            sem((tile_count, 2)),
            sem((tile_count,)),
            sem((tile_count,)),
            sem((2, BATCH, 3)),
            sem((2, BATCH)),
            sem((stages,)),
            sem((stages,)),
            sem((groups + 1,)),
            sem((groups + 1,)),
            sem((groups + 1, 2)),
            sem((groups + 1, 2)),
            sem((groups + 1, 2)),
            sem((groups + 1, 2)),
            sem((groups + 1, chips)),
            sem((groups + 1, chips)),
            sem((2,)),
            sem((2,)),
            sem((2,)),
        ],
        compiler_params=pltpu.CompilerParams(
            collective_id=2, has_side_effects=True, vmem_limit_bytes=61 * 1024 * 1024
        ),
        name="back",
    )(
        dw, ys, dx, dgates, cols, routes, tokens, grad_out, resid, normed2, normed_t, mixed_t,
        gain1, gain2, router_t, bucket_hot, wq, wo, qkv, probs,
    )


def shards(
    tokens,
    routes,
    rel_bucket,
    norm_gain1,
    w_qkv,
    w_out_proj,
    bias_table,
    norm_gain2,
    w_router,
    w_expert_in,
    w_expert_out,
    grad_out,
):
    row_count, model_width = tokens.shape
    bucket_count, head_count = bias_table.shape
    expert_count = lax.axis_size("expert")
    capacity = 10 * row_count // (4 * expert_count)
    slot_total = expert_count * capacity
    hidden_groups = 4
    shard_rows = w_qkv.shape[0]
    ws = w_qkv.reshape(shard_rows, 3, hidden_groups, -1).transpose(2, 0, 1, 3)
    ws = ws.reshape(hidden_groups, shard_rows, -1)

    bucket_ids = jnp.arange(bucket_count, dtype=jnp.int32)
    bucket_hot = jnp.concatenate(
        [bucket_ids[:, None] == rel_bucket[None, :], jnp.zeros((bucket_count, 1), bool)], axis=1
    ).astype(F32)
    table = jnp.dot(bias_table.T, bucket_hot, precision=HIGHEST)

    wq_full, out_full, qkv, probs, g_rows, mixed_t, normed1_t, residual, normed2_r, xs, gates, cols = front(
        tokens,
        norm_gain1[None],
        norm_gain2[None],
        table,
        routes,
        grad_out,
        w_router,
        ws,
        w_out_proj,
        lax.axis_size("dp"),
        capacity,
    )
    produced, grad_rows, grad_gates, grad_w = experts(
        xs, gates, g_rows, w_expert_in[0], w_expert_out[0], lax.axis_size("dp")
    )
    grad_w, _, _, small, grad_qkv, grad_out_proj, block_out, grad_tokens = back(
        grad_w,
        produced,
        grad_rows,
        grad_gates,
        cols,
        routes,
        tokens,
        grad_out,
        residual,
        normed2_r,
        normed1_t,
        mixed_t,
        norm_gain1[None],
        norm_gain2[None],
        jnp.pad(w_router.T, ((0, 128 - expert_count), (0, 0))),
        bucket_hot.astype(BF16),
        wq_full.reshape(hidden_groups, model_width, -1),
        out_full.reshape(model_width, model_width),
        qkv,
        probs,
    )
    grad_expert_in, grad_expert_out = grad_w[None, :2], grad_w[2].T[None]
    grad_qkv = grad_qkv.reshape(hidden_groups, shard_rows, 3, -1).transpose(1, 2, 0, 3)
    grad_qkv = grad_qkv.reshape(shard_rows, 3 * model_width)
    grad_router_all = small[:expert_count].T
    grad_norm1, grad_norm2 = small[expert_count], small[expert_count + 1]
    grad_bias = small[expert_count + 2 : expert_count + 2 + head_count, :bucket_count].T
    return (
        block_out,
        grad_tokens,
        grad_norm1,
        grad_qkv,
        grad_out_proj,
        grad_bias,
        grad_norm2,
        grad_router_all,
        grad_expert_in,
        grad_expert_out,
    )


def solution(mesh):
    split = P(("dp", "expert"), None)
    in_specs = (
        split,
        split,
        P(),
        P(),
        split,
        split,
        P(),
        P(),
        P(),
        P("expert", None, None, None),
        P("expert", None, None),
        split,
    )
    out_specs = (
        split,
        split,
        P(),
        split,
        split,
        P(),
        P(),
        P(),
        P("expert", None, "dp", None),
        P("expert", None, "dp"),
    )
    return jax.shard_map(shards, mesh=mesh, in_specs=in_specs, out_specs=out_specs, check_vma=False)
```

time: 973 us -> 487 us (0.50)
  waiting for transfers between devices: 532 us -> 0 us
  Pallas kernels: 32 us -> 445 us
  matrix products: 179 us -> 0.79 us
  blocking collectives: 166 us -> 0 us
  other arithmetic: 24.4 us -> 1.36 us
  local copies, waits for them, and re-layouts: 9.04 us -> 29.4 us
  between operations: 14.8 us -> 1.15 us
  starting transfers between devices: 9.78 us -> 0 us
    pallas_call x2 -> x3, Pallas kernels: 32 us -> 445 us  [the longest x1 222 us: back(): pl.pallas_call(back_kernel, in_specs=[ANY] * 2 + [vmem] * 14 + [ANY, vmem...]
    reduce_scatter x4 -> x0, waiting for transfers between devices: 308 us -> none  [the longest x1 118 us: shards(): lax.psum_scatter(grad_qkv_w.astype(BF16), ('dp', 'expert'), scatter_dimen...]
    dot_general x26 -> x0, matrix products: 178 us -> none  [the longest x17 113 us: dot_nn(): return jnp.dot(a, b, preferred_element_type=F32)]
    all_to_all x2 -> x0, blocking collectives: 128 us -> none  [exchange(): lax.all_to_all(rows.reshape(expert_count, capacity, model_width), 'expert...]
    all_to_all x2 -> x0, waiting for transfers between devices: 118 us -> none  [exchange(): lax.all_to_all(rows.reshape(expert_count, capacity, model_width), 'expert...]
    all_gather x2 -> x0, waiting for transfers between devices: 104 us -> none  [the longest x1 69.7 us: shards(): qkv_full = lax.all_gather(w_qkv, ('dp', 'expert'), axis=0, tiled=True)]
    psum x1 -> x0, blocking collectives: 38 us -> none  [shards(): lax.psum((grad_bias_local, grad_gain1, grad_gain2, grad_router), ('dp', '...]
    convert_element_type x5 -> x1, other arithmetic: 11.4 us -> 0.64 us  [shards(): bucket_hot.astype(BF16)]
  transfers between devices with their start and end apart: 8 -> 0, of which waited for: 8 -> 0; matrix products, arithmetic and copies ran while one was open for 8% -> 0% of each run, Pallas kernels for 3% -> 0%
where the time goes in v3:
time: 487 us; the launch traced here: 478 us
  Pallas kernels  445 us (91%)
  local copies, waits for them, and re-layouts  29.4 us (6%)
    pallas_call x1, Pallas kernels, back(): pl.pallas_call(back_kernel, in_specs=[ANY] * 2 + [vmem] * 14 + [ANY, vmem...  222 us
    pallas_call x1, Pallas kernels, experts(): pl.pallas_call(experts_kernel, in_specs=[ANY] * 5, out_specs=[ANY] * 4, o...  127 us
    pallas_call x1, Pallas kernels, front(): pl.pallas_call(front_kernel, in_specs=[vmem] * 9, out_specs=[ANY] * 5 + [...  95.9 us
    unnamed x12, local copies, waits for them, and re-layouts  11.6 us

profile of v3, /device:TPU:0, one launch (start us, length us, event | category | flops | bytes accessed | tf_op | source)
XLA Modules:
  0.0 477.6 jit_solution(9139262239995695491)
XLA Ops:
  0.6 0.0 copy-start
  0.7 0.7 iota_compare_fusion
  1.4 0.6 convert_convert_fusion.bucket_hot_ref
  2.0 0.0 copy-done
  2.0 0.8 convolution_bitcast_fusion.table_ref
  2.8 1.1 reshape.39
  3.9 0.1 copy.40
  4.0 0.9 reshape.40.ws_ref
  4.9 1.5 copy.34.routes_ref
  6.4 1.6 pad.5.router_t_ref
  8.0 1.8 copy.35.router_ref
  9.8 95.9 %front.1 = (bf16[4,2,2,4,2,32,768]{6,5,4,3,2,1,0:T(8,128)(2,1)}, bf16[2,2,4,2,32,1024]{5,4,3,2,1,0:T(8,128)(2,1)}, bf16[4,512,768]{2,1,0:T(8,128)(2,1)}, bf16[16...) custom-call(bf16[512,1024]{1,0:T(8,128)(2,1)} %tokens_ref.3, ...), custom_call_target="tpu_custom_call" | custom-call | tf_op jit(solution)/shard_map/front/pallas_call | solution.py:613
  105.7 127.0 %experts.1 = (bf16[8,160,1024]{2,1,0:T(8,128)(2,1)}, bf16[8,160,1024]{2,1,0:T(8,128)(2,1)}, f32[8,8,256]{2,1,0:T(8,128)}, bf16[33,4,256,256]{3,2,1,0:T(8,128)(2,1)}) custom-call(bf16[8,160,1024]{2,1,0:T(8,128)(2,1)} %get-tuple-element.32.xs_ref, f32[8,8,256]{2,1,0:T(8,128)} %get-tuple-element.33.gates_ref, bf16[8,160,1024]{2,1,0:T(8,128)(2,1)} %get-tuple-element.34.g_ref, ...), custom_call_target="tpu_custom_call" | custom-call | tf_op jit(solution)/shard_map/experts/pallas_call | solution.py:285
  232.7 222.0 %back.1 = (f32[3,256,2816]{2,1,0:T(8,128)}, bf16[33,2,256,256]{3,2,1,0:T(8,128)(2,1)}, bf16[33,256,256]{2,1,0:T(8,128)(2,1)}, f32[32,1024]{1,0:T(8,128)}, f32[4,...) custom-call(bf16[33,4,256,256]{3,2,1,0:T(8,128)(2,1)} %get-tuple-element.35.dw_ref, ...), custom_call_target="tpu_custom_call" | custom-call | tf_op jit(solution)/shard_map/back/pallas_call | solution.py:1254
  454.7 1.3 slice_bitcast_fusion.3
  456.0 1.4 fusion.2
  457.5 1.4 slice_bitcast_fusion.2
  458.8 1.2 reshape.43
  460.0 0.3 copy.37
  460.3 0.9 reshape.44
  461.2 2.0 slice_bitcast_fusion.1
  463.2 5.5 %slice_bitcast_fusion = f32[1,2,256,2816]{3,2,1,0:T(8,128)} fusion(f32[3,256,2816]{2,1,0:T(8,128)} %get-tuple-element.53), kind=kLoop, calls=%fused_computation | loop fusion | bytes 11534336 | tf_op jit(solution)/shard_map/broadcast_in_dim | solution.py:1388
  468.8 0.0 copy-start.1
  468.8 2.2 copy.38
  471.0 0.0 copy-start.2
  471.0 2.3 copy.47
  473.3 3.2 copy.48
  476.5 0.0 copy-done.2
  476.5 0.7 copy.49
  477.1 0.0 copy-done.1
Async XLA Ops:
  0.6 1.4 copy-start
  468.8 8.3 %copy-start.1 = (f32[32,16]{0,1:T(8,128)S(1)}, f32[32,16]{0,1:T(8,128)}, u32[]{:S(2)}) copy-start(f32[32,16]{0,1:T(8,128)} %param.18) | copy-start | bytes 6148
  471.0 5.5 %copy-start.2 = (f32[32,1024]{1,0:T(8,128)S(1)}, f32[32,1024]{1,0:T(8,128)}, u32[]{:S(2)}) copy-start(f32[32,1024]{1,0:T(8,128)} %get-tuple-element.100) | copy-start | bytes 393220
